TPU v7x, 32 devices: a whole 2x2x4 slice. The times are simulated.
32 devices in a mesh: row: 4 (over y, x), col: 8 (over z, core).
Axes of the slice: x: 2, y: 2, z: 4, core: 2. Of those that a mesh axis runs over, the one named last changes fastest.
Arguments:
- g_start: float32 [2048, 32768], P('row', 'col'), may hold values from -6 to 6
- cotangent: float32 [2048, 32768], P('row', 'col'), may hold values from -6 to 6
- damping: float32 [32768], replicated, may hold values from 0.1 to 3
- hopping: float32 [6, 32768], replicated, may hold values from -4 to 4
- bonds: int32 [7, 32768], replicated, may hold values 0 or 1
- source: float32 [7, 32768], replicated, may hold values from -5 to 5
Outputs:
- g_end: float32 [2048, 32768], P('row', 'col')
- g_adjoint: float32 [2048, 32768], P('row', 'col')
All inputs are finite; a program needn't handle non-finite values.
Results may differ from a plain program's by a relative error of at most 0.00002.
Values sent between devices are 32-bit elements; how exact they have to be, the bound alone decides.
No kernel may reach another device: no remote copies, remote signals or barrier semaphores. Data moves between devices by JAX's collectives and lax.ppermute only.
A program may use at most 192 MiB of HBM per device.

v0:
```python
import jax
import jax.numpy as jnp
from jax import lax
from jax.sharding import PartitionSpec as P

LX = 128


DT = 0.1


def padded(cells, sides, width, closed):
    for axis, dim in sides:
        count = lax.axis_size(axis)
        ends = count if closed else count - 1
        head = lax.slice_in_dim(cells, 0, width, axis=dim)
        tail = lax.slice_in_dim(cells, cells.shape[dim] - width, cells.shape[dim], axis=dim)
        cells = jnp.concatenate(
            [
                lax.ppermute(tail, axis, [(i, (i + 1) % count) for i in range(ends)]),
                cells,
                lax.ppermute(head, axis, [((i + 1) % count, i) for i in range(ends)]),
            ],
            axis=dim,
        )
    return cells


def band_offsets(side):
    return (0, 1, -1, 2, -2, 2 * side, -2 * side)


def apart_faces(block, width):
    rows_ext = padded(block, (("row", 0),), width, False)
    cols_ext = padded(block, (("col", 1),), width, True)
    return (rows_ext, cols_ext)


def shards(g_start, cotangent, damping, hopping, bonds, source):
    rows_dev, cols_dev = g_start.shape
    modes = damping.shape[0]
    reach = 2 * LX
    offsets = band_offsets(LX)
    row_first = lax.axis_index("row") * rows_dev
    col_first = lax.axis_index("col") * cols_dev
    coef = jnp.concatenate([-damping[None, :], hopping], axis=0) * bonds.astype(jnp.float32)
    coef_rows = jnp.pad(coef, ((0, 0), (2 * reach, 2 * reach)))
    coef_cols = jnp.concatenate([coef[:, modes - 2 * reach :], coef, coef[:, : 2 * reach]], axis=1)
    source_rows = jnp.pad(source, ((0, 0), (2 * reach, 2 * reach)))

    def forward_rate(rows_ext, cols_ext, out_row, out_col):
        count_rows = cols_ext.shape[0]
        count_cols = rows_ext.shape[1]
        band_rows = lax.dynamic_slice_in_dim(coef_rows, out_row + 2 * reach, count_rows, 1)
        band_cols = lax.dynamic_slice_in_dim(coef_cols, out_col + 2 * reach, count_cols, 1)
        feed_rows = lax.dynamic_slice_in_dim(source_rows, out_row + 2 * reach, count_rows, 1)
        glob_rows = out_row + lax.iota(jnp.int32, count_rows)
        glob_cols = jnp.mod(out_col + lax.iota(jnp.int32, count_cols), modes)
        rate = jnp.zeros((count_rows, count_cols), jnp.float32)
        for index, offset in enumerate(offsets):
            rate = (
                rate
                + band_rows[index][:, None]
                * rows_ext[reach + offset : reach + offset + count_rows, :]
            )
            rate = (
                rate
                + cols_ext[:, reach + offset : reach + offset + count_cols]
                * band_cols[index][None, :]
            )
            target = jnp.mod(glob_rows + offset, modes)
            rate = rate + jnp.where(
                glob_cols[None, :] == target[:, None], feed_rows[index][:, None], 0.0
            )
        return rate

    def adjoint_rate(rows_ext, cols_ext, out_row, out_col):
        count_rows = cols_ext.shape[0]
        count_cols = rows_ext.shape[1]
        band_rows = lax.dynamic_slice_in_dim(coef_rows, out_row + reach, count_rows + 2 * reach, 1)
        band_cols = lax.dynamic_slice_in_dim(coef_cols, out_col + reach, count_cols + 2 * reach, 1)
        rate = jnp.zeros((count_rows, count_cols), jnp.float32)
        for index, offset in enumerate(offsets):
            weighted_rows = rows_ext * band_rows[index][:, None]
            rate = rate + weighted_rows[reach - offset : reach - offset + count_rows, :]
            weighted_cols = cols_ext * band_cols[index][None, :]
            rate = rate + weighted_cols[:, reach - offset : reach - offset + count_cols]
        return rate

    def extend(block):
        return apart_faces(block, reach)

    def advance(block, rate_fn):
        rows_ext, cols_ext = extend(block)
        first_rate = rate_fn(rows_ext, cols_ext, row_first, col_first)
        middle = block + 0.5 * DT * first_rate
        rows_mid, cols_mid = extend(middle)
        second_rate = rate_fn(rows_mid, cols_mid, row_first, col_first)
        return block + DT * second_rate

    g_end = advance(g_start, forward_rate)
    g_adjoint = advance(cotangent, adjoint_rate)
    return (g_end, g_adjoint)


def solution(mesh):
    return jax.shard_map(
        shards,
        mesh=mesh,
        in_specs=(P("row", "col"), P("row", "col"), P(), P(), P(), P()),
        out_specs=(P("row", "col"), P("row", "col")),
        check_vma=False,
    )
```

profile of v0, /device:TPU:0, one launch (start us, length us, event | category | flops | bytes accessed | tf_op | source)
XLA Modules:
  0.0 785.4 jit_solution(17754912826005807334)
XLA Ops:
  0.6 0.0 copy-start
  0.6 8.0 %fusion.93 = (f32[256,4096]{1,0:T(8,128)}, f32[256,4096]{1,0:T(8,128)}) fusion(f32[512,4096]{1,0:T(8,128)} %param.6), kind=kLoop, calls=%fused_computation.242 | loop fusion | bytes 16777216 | tf_op jit(solution)/shard_map/slice | solution.py:16
  8.6 6.8 collective-permute-start.2
  15.4 2.2 fusion.94
  17.6 0.1 collective-permute-start.3
  17.7 3.9 fusion.89
  21.5 3.6 collective-permute-start.8
  25.1 1.1 fusion.90
  26.2 1.5 collective-permute-start.10
  27.7 1.3 collective-permute-start.9
  29.0 0.3 maximum_multiply_fusion
  29.3 0.1 pad_maximum_fusion.6
  29.4 0.4 dynamic-slice_reduce_fusion.6
  29.9 0.1 pad_dynamic-slice_fusion.12
  30.1 0.1 slice.532
  30.1 0.1 slice.530
  30.2 0.1 slice.528
  30.3 0.1 slice.526
  30.4 0.1 slice.524
  30.4 0.1 slice.522
  30.5 0.1 slice.520
  30.6 0.1 slice.518
  30.7 0.1 pad_dynamic-slice_fusion.18
  30.8 0.1 pad_dynamic-slice_fusion.5
  31.0 0.3 constant_dynamic-slice_fusion
  31.3 2.1 collective-permute-start.1
  33.4 1.9 constant_dynamic-update-slice_fusion.7
  35.3 1.8 collective-permute-done.10
  37.0 1.3 collective-permute-start
  38.3 1.9 constant_dynamic-update-slice_fusion.13
  40.2 153.2 %collective-permute-done.8 = f32[256,4096]{1,0:T(8,128)} collective-permute-done((f32[256,4096]{1,0:T(8,128)}, f32[256,4096]{1,0:T(8,128)}, u32[]{:S(2)}, u32[]{:S(2)}) %collective-permute-start.8) | collective-permute-done | bytes 4194336 | tf_op jit(solution)/shard_map/ppermute | solution.py:20
  193.4 2.2 collective-permute-start.11
  195.6 4.6 constant_dynamic-update-slice_fusion.10
  200.2 11.3 %constant_dynamic-update-slice_fusion.9 = (f32[1024,4096]{1,0:T(8,128)}, f32[512,4608]{1,0:T(8,128)}) fusion(f32[1024,4096]{1,0:T(8,128)} %constant_dynamic-update-slice_fusion.10, f32[512,4096]{1,0:T(8,128)} %param.7, f32[512,4608]{1,0:T(8,128)} %constant_dynamic-update-slice_fusion.13), kind=kLoop, calls=%fused_computation.187 | loop fusion | bytes 25165824
  211.5 0.0 collective-permute-done.11
  211.5 0.9 constant_dynamic-update-slice_fusion.11
  212.4 74.0 %collective-permute-done.9 = f32[256,4096]{1,0:T(8,128)} collective-permute-done((f32[256,4096]{1,0:T(8,128)}, f32[256,4096]{1,0:T(8,128)}, u32[]{:S(2)}, u32[]{:S(2)}) %collective-permute-start.9) | collective-permute-done | bytes 4194336 | tf_op jit(solution)/shard_map/ppermute | solution.py:22
  286.4 4.6 constant_dynamic-update-slice_fusion.8
  291.0 55.6 %fusion.59 = f32[512,4096]{1,0:T(8,128)} fusion(f32[512,4096]{1,0:T(8,128)} %param.7, f32[512,4608]{1,0:T(8,128)} %constant_dynamic-update-slice_fusion.11, f32[1024,4096]{1,0:T(8,128)} %constant_dynamic-update-slice_fusion.8, f32[4096]{0:T(1024)S(1)} %slice.540, f32[512]{0:T(512)S(1)} %slice.538, f32[4096]{0:T(1024)S(1)} %slice.536, f32[512]{0:T(512)S(1)} %slice.534, ...), kind=kLoop, calls=%fused_computation.108 | loop fusion | flops 60817408 | bytes 134346752 | tf_op jit(solution)/shard_map/add | solution.py:96
  346.6 1.3 fusion.88
  347.9 1.1 collective-permute-start.15
  348.9 0.0 collective-permute-start.14
  348.9 7.9 %fusion.87 = (f32[256,4096]{1,0:T(8,128)}, f32[256,4096]{1,0:T(8,128)}) fusion(f32[512,4096]{1,0:T(8,128)} %fusion.59), kind=kLoop, calls=%fused_computation.236 | loop fusion | bytes 16777216 | tf_op jit(solution)/shard_map/slice | solution.py:17
  356.9 1.3 collective-permute-start.13
  358.2 4.6 constant_dynamic-update-slice_fusion.5
  362.8 12.7 %constant_dynamic-update-slice_fusion.1 = (f32[768,4096]{1,0:T(8,128)}, f32[768,4096]{1,0:T(8,128)}, f32[512,4352]{1,0:T(8,128)}, f32[512,4352]{1,0:T(8,128)}) fusion(f32[512,4096]{1,0:T(8,128)S(1)} %bitcast.30, f32[768,4096]{1,0:T(8,128)} %constant_dynamic-update-slice_fusion.5, f32[512,4352]{1,0:T(8,128)} %constant_dynamic-update-slice_fusion.7), kind=kLoop, calls=%fused_computation.179 | loop fusion | bytes 41943040
  375.4 6.7 collective-permute-start.12
  382.1 0.9 constant_dynamic-update-slice_fusion.2
  383.0 4.6 constant_dynamic-update-slice_fusion
  387.6 39.0 %fusion.32 = f32[512,4096]{1,0:T(8,128)} fusion(f32[512,4096]{1,0:T(8,128)} %param.6, f32[512,4352]{1,0:T(8,128)} %get-tuple-element.28, f32[768,4096]{1,0:T(8,128)} %get-tuple-element.26, f32[512,4352]{1,0:T(8,128)} %constant_dynamic-update-slice_fusion.2, f32[768,4096]{1,0:T(8,128)} %constant_dynamic-update-slice_fusion, f32[512]{0:T(512)S(1)} %bitcast.72, ...), kind=kLoop, calls=%fused_computation.66 | loop fusion | flops 102760448 | bytes 117614592 | tf_op jit(solution)/shard_map/add | solution.py:96
  426.7 7.9 %fusion.91 = (f32[256,4096]{1,0:T(8,128)}, f32[256,4096]{1,0:T(8,128)}) fusion(f32[512,4096]{1,0:T(8,128)} %fusion.32), kind=kLoop, calls=%fused_computation.240 | loop fusion | bytes 16777216 | tf_op jit(solution)/shard_map/slice | solution.py:16
  434.6 2.1 fusion.92
  436.7 0.6 collective-permute-start.7
  437.3 4.3 collective-permute-start.6
  441.6 1.3 collective-permute-start.4
  442.9 8.4 %pad_maximum_fusion.1 = f32[512,4608]{1,0:T(8,128)} fusion(f32[512,256]{1,0:T(8,128)S(1)} %collective-permute-done.15, f32[512,4096]{1,0:T(8,128)} %fusion.59, f32[512,256]{1,0:T(8,128)S(1)} %collective-permute-done.14), kind=kLoop, calls=%fused_computation.29 | loop fusion | flops 4718592 | bytes 18874368 | tf_op jit(solution)/shard_map/concatenate | solution.py:18
  451.3 14.9 %collective-permute-done.13 = f32[256,4096]{1,0:T(8,128)} collective-permute-done((f32[256,4096]{1,0:T(8,128)}, f32[256,4096]{1,0:T(8,128)}, u32[]{:S(2)}, u32[]{:S(2)}) %collective-permute-start.13) | collective-permute-done | bytes 4194336 | tf_op jit(solution)/shard_map/ppermute | solution.py:22
  466.2 1.0 collective-permute-start.5
  467.2 4.0 collective-permute-done.12
  471.3 11.8 %pad_maximum_fusion = f32[1024,4096]{1,0:T(8,128)} fusion(f32[256,4096]{1,0:T(8,128)} %collective-permute-done.13, f32[512,4096]{1,0:T(8,128)} %fusion.59, f32[256,4096]{1,0:T(8,128)} %collective-permute-done.12), kind=kLoop, calls=%fused_computation | loop fusion | flops 8388608 | bytes 33554432 | tf_op jit(solution)/shard_map/concatenate | solution.py:18
  483.0 55.6 %fusion.44 = f32[512,4096]{1,0:T(8,128)} fusion(f32[512,4096]{1,0:T(8,128)} %param.7, f32[512,4608]{1,0:T(8,128)} %pad_maximum_fusion.1, f32[1024,4096]{1,0:T(8,128)} %pad_maximum_fusion, f32[4096]{0:T(1024)S(1)} %slice.540, f32[512]{0:T(512)S(1)} %slice.538, f32[4096]{0:T(1024)S(1)} %slice.536, f32[512]{0:T(512)S(1)} %slice.534, f32[4096]{0:T(1024)S(1)} %slice.532, ...), kind=kLoop, calls=%fused_computation.79 | loop fusion | flops 60817408 | bytes 134346752 | tf_op jit(solution)/shard_map/add | solution.py:99
  538.6 22.4 %collective-permute-done.6 = f32[256,4096]{1,0:T(8,128)} collective-permute-done((f32[256,4096]{1,0:T(8,128)}, f32[256,4096]{1,0:T(8,128)}, u32[]{:S(2)}, u32[]{:S(2)}) %collective-permute-start.6) | collective-permute-done | bytes 4194336 | tf_op jit(solution)/shard_map/ppermute | solution.py:20
  561.1 173.6 %collective-permute-done.4 = f32[256,4096]{1,0:T(8,128)} collective-permute-done((f32[256,4096]{1,0:T(8,128)}, f32[256,4096]{1,0:T(8,128)}, u32[]{:S(2)}, u32[]{:S(2)}) %collective-permute-start.4) | collective-permute-done | bytes 4194336 | tf_op jit(solution)/shard_map/ppermute | solution.py:22
  734.7 50.6 %multiply_add_fusion = f32[512,4096]{1,0:T(8,128)} fusion(f32[512,4096]{1,0:T(8,128)} %param.6, f32[512,4096]{1,0:T(8,128)} %fusion.32, f32[512,256]{1,0:T(8,128)S(1)} %collective-permute-done.7, f32[256,4096]{1,0:T(8,128)} %collective-permute-done.6, f32[512,256]{1,0:T(8,128)S(1)} %collective-permute-done.5, f32[256,4096]{1,0:T(8,128)} %collective-permute-done.4, ...), kind=kLoop, calls=%fused_computation.154 | loop fusion | flops 127926272 | bytes 34777088 | tf_op jit(solution)/shard_map/add | solution.py:99
  (35 shorter events, 0.1 us)
Async XLA Ops:
  0.6 17.0 %copy-start = (f32[512,4096]{1,0:T(8,128)S(1)}, f32[512,4096]{1,0:T(8,128)}, u32[]{:S(2)}) copy-start(f32[512,4096]{1,0:T(8,128)} %param.7) | copy-start | bytes 25165828
  8.6 348.3 %collective-permute-start.2 = (f32[256,4096]{1,0:T(8,128)}, f32[256,4096]{1,0:T(8,128)}, u32[]{:S(2)}, u32[]{:S(2)}) collective-permute-start(f32[256,4096]{1,0:T(8,128)} %get-tuple-element.24), channel_id=1, source_target_pairs={{0,8},{8,16},{16,24},{1,9},{9,17},{17,25},{2,10},{10,18},{18,26},{... | collective-permute-start | bytes 12582920 | tf_op jit(solution)/shard_map/ppermute | solution.py:20
  17.6 11.4 %copy-start.4 = (f32[32768]{0:T(1024)S(1)}, f32[32768]{0:T(1024)}, u32[]{:S(2)}) copy-start(f32[32768]{0:T(1024)} %param.8) | copy-start | bytes 393220
  17.6 11.4 %copy-start.1 = (f32[6,32768]{1,0:T(8,128)S(1)}, f32[6,32768]{1,0:T(8,128)}, u32[]{:S(2)}) copy-start(f32[6,32768]{1,0:T(8,128)} %param.9) | copy-start | bytes 2359300
  17.6 11.4 %copy-start.2 = (s32[7,32768]{1,0:T(8,128)S(1)}, s32[7,32768]{1,0:T(8,128)}, u32[]{:S(2)}) copy-start(s32[7,32768]{1,0:T(8,128)} %param.10) | copy-start | bytes 2752516
  17.6 13.7 %collective-permute-start.3 = (f32[512,256]{1,0:T(8,128)}, f32[512,256]{1,0:T(8,128)}, u32[]{:S(2)}, u32[]{:S(2)}) collective-permute-start(f32[512,256]{1,0:T(8,128)} %get-tuple-element.30), channel_id=1, source_target_pairs={{0,1},{1,2},{2,3},{3,4},{4,5},{5,6},{6,7},{7,0},{8,9},{9,10},{10,1... | collective-permute-start | bytes 1572872 | tf_op jit(solution)/shard_map/ppermute | solution.py:20
  21.5 9.3 %copy-start.3 = (f32[7,32768]{1,0:T(8,128)S(1)}, f32[7,32768]{1,0:T(8,128)}, u32[]{:S(2)}) copy-start(f32[7,32768]{1,0:T(8,128)} %param.11) | copy-start | bytes 2752516
  21.5 171.9 %collective-permute-start.8 = (f32[256,4096]{1,0:T(8,128)}, f32[256,4096]{1,0:T(8,128)}, u32[]{:S(2)}, u32[]{:S(2)}) collective-permute-start(f32[256,4096]{1,0:T(8,128)} %get-tuple-element.14), channel_id=1, source_target_pairs={{0,8},{8,16},{16,24},{1,9},{9,17},{17,25},{2,10},{10,18},{18,26},{... | collective-permute-start | bytes 12582920 | tf_op jit(solution)/shard_map/ppermute | solution.py:20
  26.2 10.9 %collective-permute-start.10 = (f32[512,256]{1,0:T(8,128)}, f32[512,256]{1,0:T(8,128)}, u32[]{:S(2)}, u32[]{:S(2)}) collective-permute-start(f32[512,256]{1,0:T(8,128)} %get-tuple-element.18), channel_id=1, source_target_pairs={{0,1},{1,2},{2,3},{3,4},{4,5},{5,6},{6,7},{7,0},{8,9},{9,10},{10,1... | collective-permute-start | bytes 1572872 | tf_op jit(solution)/shard_map/ppermute | solution.py:20
  27.7 258.7 %collective-permute-start.9 = (f32[256,4096]{1,0:T(8,128)}, f32[256,4096]{1,0:T(8,128)}, u32[]{:S(2)}, u32[]{:S(2)}) collective-permute-start(f32[256,4096]{1,0:T(8,128)} %get-tuple-element.13), channel_id=1, source_target_pairs={{8,0},{16,8},{24,16},{9,1},{17,9},{25,17},{10,2},{18,10},{26,18},{... | collective-permute-start | bytes 12582920 | tf_op jit(solution)/shard_map/ppermute | solution.py:22
  31.3 344.2 %collective-permute-start.1 = (f32[512,256]{1,0:T(8,128)}, f32[512,256]{1,0:T(8,128)S(1)}, u32[]{:S(2)}, u32[]{:S(2)}) collective-permute-start(f32[512,256]{1,0:T(8,128)} %get-tuple-element.29), channel_id=1, source_target_pairs={{1,0},{2,1},{3,2},{4,3},{5,4},{6,5},{7,6},{0,7},{9,8},{10,9},{11,1... | collective-permute-start | bytes 1572872 | tf_op jit(solution)/shard_map/ppermute | solution.py:22
  37.0 346.0 %collective-permute-start = (f32[256,4096]{1,0:T(8,128)}, f32[256,4096]{1,0:T(8,128)}, u32[]{:S(2)}, u32[]{:S(2)}) collective-permute-start(f32[256,4096]{1,0:T(8,128)} %get-tuple-element.23), channel_id=1, source_target_pairs={{8,0},{16,8},{24,16},{9,1},{17,9},{25,17},{10,2},{18,10},{26,18},{... | collective-permute-start | bytes 12582920 | tf_op jit(solution)/shard_map/ppermute | solution.py:22
  193.4 18.1 %collective-permute-start.11 = (f32[512,256]{1,0:T(8,128)}, f32[512,256]{1,0:T(8,128)S(1)}, u32[]{:S(2)}, u32[]{:S(2)}) collective-permute-start(f32[512,256]{1,0:T(8,128)} %get-tuple-element.17), channel_id=1, source_target_pairs={{1,0},{2,1},{3,2},{4,3},{5,4},{6,5},{7,6},{0,7},{9,8},{10,9},{11,1... | collective-permute-start | bytes 1572872 | tf_op jit(solution)/shard_map/ppermute | solution.py:22
  347.9 89.4 %collective-permute-start.15 = (f32[512,256]{1,0:T(8,128)S(1)}, f32[512,256]{1,0:T(8,128)S(1)}, u32[]{:S(2)}, u32[]{:S(2)}) collective-permute-start(f32[512,256]{1,0:T(8,128)S(1)} %get-tuple-element.12), channel_id=1, source_target_pairs={{1,0},{2,1},{3,2},{4,3},{5,4},{6,5},{7,6},{0,7},{9,8},{10,9},{11,1... | collective-permute-start | bytes 1572872 | tf_op jit(solution)/shard_map/ppermute | solution.py:22
  348.9 13.8 %slice-start = ((s8[8388608]{0:T(1024)(128)(4,1)}), s8[4194304]{0:T(1024)(128)(4,1)S(1)}, s32[]{:S(2)}) async-start(s8[8388608]{0:T(1024)(128)(4,1)} %bitcast.29), calls=%async_computation | async-start | bytes 8388608
  348.9 13.8 %slice-start.1 = ((s8[8388608]{0:T(1024)(128)(4,1)}), s8[4194304]{0:T(1024)(128)(4,1)S(1)}, s32[]{:S(2)}) async-start(s8[8388608]{0:T(1024)(128)(4,1)} %bitcast.29), calls=%async_computation.1 | async-start | bytes 8388608
  348.9 92.6 %collective-permute-start.14 = (f32[512,256]{1,0:T(8,128)S(1)}, f32[512,256]{1,0:T(8,128)S(1)}, u32[]{:S(2)}, u32[]{:S(2)}) collective-permute-start(f32[512,256]{1,0:T(8,128)S(1)} %get-tuple-element.11), channel_id=1, source_target_pairs={{0,1},{1,2},{2,3},{3,4},{4,5},{5,6},{6,7},{7,0},{8,9},{9,10},{10,1... | collective-permute-start | bytes 1572872 | tf_op jit(solution)/shard_map/ppermute | solution.py:20
  356.9 109.3 %collective-permute-start.13 = (f32[256,4096]{1,0:T(8,128)}, f32[256,4096]{1,0:T(8,128)}, u32[]{:S(2)}, u32[]{:S(2)}) collective-permute-start(f32[256,4096]{1,0:T(8,128)} %get-tuple-element.10), channel_id=1, source_target_pairs={{8,0},{16,8},{24,16},{9,1},{17,9},{25,17},{10,2},{18,10},{26,18},{... | collective-permute-start | bytes 12582920 | tf_op jit(solution)/shard_map/ppermute | solution.py:22
  375.4 95.8 %collective-permute-start.12 = (f32[256,4096]{1,0:T(8,128)}, f32[256,4096]{1,0:T(8,128)}, u32[]{:S(2)}, u32[]{:S(2)}) collective-permute-start(f32[256,4096]{1,0:T(8,128)} %get-tuple-element.9), channel_id=1, source_target_pairs={{0,8},{8,16},{16,24},{1,9},{9,17},{17,25},{2,10},{10,18},{18,26},{... | collective-permute-start | bytes 12582920 | tf_op jit(solution)/shard_map/ppermute | solution.py:20
  436.7 101.9 %collective-permute-start.7 = (f32[512,256]{1,0:T(8,128)}, f32[512,256]{1,0:T(8,128)S(1)}, u32[]{:S(2)}, u32[]{:S(2)}) collective-permute-start(f32[512,256]{1,0:T(8,128)} %get-tuple-element.22), channel_id=1, source_target_pairs={{0,1},{1,2},{2,3},{3,4},{4,5},{5,6},{6,7},{7,0},{8,9},{9,10},{10,1... | collective-permute-start | bytes 1572872 | tf_op jit(solution)/shard_map/ppermute | solution.py:20
  437.3 123.8 %collective-permute-start.6 = (f32[256,4096]{1,0:T(8,128)}, f32[256,4096]{1,0:T(8,128)}, u32[]{:S(2)}, u32[]{:S(2)}) collective-permute-start(f32[256,4096]{1,0:T(8,128)} %get-tuple-element.20), channel_id=1, source_target_pairs={{0,8},{8,16},{16,24},{1,9},{9,17},{17,25},{2,10},{10,18},{18,26},{... | collective-permute-start | bytes 12582920 | tf_op jit(solution)/shard_map/ppermute | solution.py:20
  441.6 293.1 %collective-permute-start.4 = (f32[256,4096]{1,0:T(8,128)}, f32[256,4096]{1,0:T(8,128)}, u32[]{:S(2)}, u32[]{:S(2)}) collective-permute-start(f32[256,4096]{1,0:T(8,128)} %get-tuple-element.19), channel_id=1, source_target_pairs={{8,0},{16,8},{24,16},{9,1},{17,9},{25,17},{10,2},{18,10},{26,18},{... | collective-permute-start | bytes 12582920 | tf_op jit(solution)/shard_map/ppermute | solution.py:22
  466.2 72.4 %collective-permute-start.5 = (f32[512,256]{1,0:T(8,128)S(1)}, f32[512,256]{1,0:T(8,128)S(1)}, u32[]{:S(2)}, u32[]{:S(2)}) collective-permute-start(f32[512,256]{1,0:T(8,128)S(1)} %get-tuple-element.21), channel_id=1, source_target_pairs={{1,0},{2,1},{3,2},{4,3},{5,4},{6,5},{7,6},{0,7},{9,8},{10,9},{11,1... | collective-permute-start | bytes 1572872 | tf_op jit(solution)/shard_map/ppermute | solution.py:22
where the time goes:
time: 786 us; the launch traced here: 785 us
  waiting for transfers between devices  444 us (56%)
  other arithmetic  221 us (28%)
  local copies, waits for them, and re-layouts  84 us (11%)
  starting transfers between devices  35 us (4%)
    ppermute x8, waiting for transfers between devices, padded(): lax.ppermute(head, axis, [((i + 1) % count, i) for i in range(ends)])  263 us
    ppermute x8, waiting for transfers between devices, padded(): lax.ppermute(tail, axis, [(i, (i + 1) % count) for i in range(ends)])  181 us
    add x2, other arithmetic, advance(): return block + DT * second_rate  106 us
    add x2, other arithmetic, advance(): middle = block + 0.5 * DT * first_rate  94.6 us
    unnamed x20, local copies, waits for them, and re-layouts  37 us
    slice x6, local copies, waits for them, and re-layouts, padded(): head = lax.slice_in_dim(cells, 0, width, axis=dim)  25.1 us
    ppermute x8, starting transfers between devices, padded(): lax.ppermute(tail, axis, [(i, (i + 1) % count) for i in range(ends)])  23.5 us
    concatenate x2, other arithmetic, padded(): jnp.concatenate([lax.ppermute(tail, axis, [(i, (i + 1) % count) for i in...  20.2 us
  transfers between devices with their start and end apart: 16, of which 7 were waited for; matrix products, arithmetic and copies ran while one was open for 31% of the time, Pallas kernels for 0%

commit v1 on v0

v1 whole, which is shorter than its diff:
```python
import functools

import jax
import jax.numpy as jnp
from jax import lax
from jax.experimental import pallas as pl
from jax.experimental.pallas import tpu as pltpu
from jax.sharding import PartitionSpec as P

LX = 128
DT = 0.1

LANES = 128
STRIP = 8
REACH = 2 * LX
HALVES = REACH // LANES
UNROLL = 64
OFFSETS = (0, 1, -1, 2, -2, REACH, -REACH)
MIRROR = (0, 2, 1, 4, 3, 6, 5)
IN_FLIGHT = 2
HOLD = 5
VMEM = 28 * 2**20


def block_rates(win, lane, count, row, coef, coef_row, band, index, put):
    lanes = lax.broadcasted_iota(jnp.int32, (STRIP, LANES), 1)
    wide = count * HALVES

    def strip(i, _):
        at = pl.multiple_of(row + i * STRIP, STRIP)
        rows_c = pl.ds(pl.multiple_of(coef_row + i * STRIP, STRIP), STRIP)
        weights = [coef[k, rows_c, :] for k in range(7)]

        def load(j, shift=0):
            return win[lane + j, pl.ds(at + shift, STRIP), :]

        line = [load(j) for j in range(-1, wide + 1)]

        def moved(shift):
            if shift > 0:
                turned = [pltpu.roll(v, LANES - shift, 1) for v in line[1:]]
                return [jnp.where(lanes < LANES - shift, turned[c], turned[c + 1]) for c in range(wide)]
            turned = [pltpu.roll(v, -shift, 1) for v in line[:-1]]
            return [jnp.where(lanes >= -shift, turned[c + 1], turned[c]) for c in range(wide)]

        by_col = {s: moved(s) for s in (1, -1, 2, -2)}
        by_col[REACH] = [load(c + HALVES) for c in range(wide)]
        by_col[-REACH] = [load(c - HALVES) for c in range(wide)]
        for c in range(wide):
            value = line[c + 1]
            total = (weights[0] + band[index + c, 0]) * value
            for k in range(1, 7):
                total = total + weights[k] * load(c, OFFSETS[k])
                total = total + band[index + c, k] * by_col[OFFSETS[k]][c]
            put(c, i, value, total)
        return 0

    lax.fori_loop(0, REACH // STRIP, strip, 0, unroll=max(UNROLL // wide, 1))


def runs(tiles):
    found = []
    for tile in tiles:
        if found and tile == found[-1][0] + found[-1][1]:
            found[-1] = (found[-1][0], found[-1][1] + 1)
        else:
            found.append((tile, 1))
    return found


def tile_kernel(plan, *refs):
    names, a_own, a_near, b, own_loads, near_loads, far_loads, mid_loads, e_first, m_first, modes, cols, fed = plan
    n_in, n_out = len(names), len(a_own) + (1 if b else 0)
    ref = dict(zip(names, refs[:n_in]))
    outs = refs[n_in : n_in + n_out]
    win, mid, coef, band, feed, sems, out_sems, feed_sems = refs[n_in + n_out :]
    base = ref["base"][0]
    row_axis = lax.axis_index("row")
    odd = lax.rem(row_axis, 2)
    block_of = {"PF": 5 - 5 * odd, "PN": 4 - 3 * odd, "QN": 1 + 3 * odd, "QF": 5 * odd}
    row_first = row_axis * (2 * REACH)
    col_first = lax.axis_index("col") * cols
    own_rows = pl.ds(2 * REACH, 2 * REACH)
    mid_rows = pl.ds(REACH, 2 * REACH)
    used = []

    def load(src, dst):
        copy = pltpu.make_async_copy(src, dst, sems.at[len(used)])
        copy.start()
        used.append(copy)
        return copy

    def pair(first):
        return pl.ds(first * HALVES, HALVES)

    def load_piece(kind, name, offset, tile, group):
        start = pl.multiple_of(block_of[kind] * REACH, REACH)
        for c in range(HALVES):
            src = ref[name].at[pl.ds((offset + c) * REACH, REACH), :]
            group.append(load(src, win.at[(tile - e_first) * HALVES + c, pl.ds(start, REACH), :]))

    band_tiles = sorted(set(a_own) | set(a_near) | set(b))
    first, second, third = [], [], []
    for name, at, from_base, tile in own_loads:
        for c in range(HALVES):
            lane = at * REACH + c * LANES
            if from_base:
                lane = pl.multiple_of(base * REACH + lane, LANES)
            src = ref[name].at[:, pl.ds(lane, LANES)]
            first.append(load(src, win.at[(tile - e_first) * HALVES + c, own_rows, :]))
    for index, tile in enumerate(band_tiles):
        src = ref["band"].at[pl.ds((base + tile + 1) * HALVES, HALVES)]
        first.append(load(src, band.at[pair(index)]))
    if a_own or b:
        first.append(load(ref["coef"].at[:, mid_rows, :], coef.at[:, mid_rows, :]))
    for kind, name, offset, tile in near_loads:
        load_piece(kind, name, offset, tile, first if tile in a_own else second)
    for kind, name, offset, tile in far_loads:
        load_piece(kind, name, offset, tile, second)
    if a_near:
        for rows in (pl.ds(0, REACH), pl.ds(3 * REACH, REACH)):
            second.append(load(ref["coef"].at[:, rows, :], coef.at[:, rows, :]))
    for name, tile in mid_loads:
        third.append(load(ref[name], mid.at[pair(tile - m_first), mid_rows, :]))

    def wait(copies):
        for copy in copies:
            copy.wait()

    feeds = {}

    def load_source(stage, tile, block):
        ahead = col_first + (base + tile) * REACH - (row_first + (block - 1) * REACH)
        ahead = lax.rem(ahead + 2 * modes, modes)
        ahead = jnp.where(ahead * 2 > modes, ahead - modes, ahead)
        hit = jnp.abs(ahead) < 2 * REACH
        which = jnp.where(ahead < 0, 0, jnp.where(ahead > 0, 2, 1))
        slot = len(feeds)
        copy = pltpu.make_async_copy(ref["feed"].at[block, which], feed.at[slot], feed_sems.at[slot])
        pl.when(hit)(copy.start)
        feeds[stage, tile, block] = hit, copy, slot

    if fed:
        for tile in a_own:
            load_source(0, tile, 1)
            load_source(0, tile, 2)
        for tile in a_near:
            load_source(0, tile, 0)
            load_source(0, tile, 3)
        for tile in b:
            load_source(1, tile, 1)
            load_source(1, tile, 2)

    def add_source(target, lane, row, stage, tile, block, step):
        hit, copy, slot = feeds[stage, tile, block]

        @pl.when(hit)
        def _():
            copy.wait()

            def strip(i, _):
                at = pl.multiple_of(i * STRIP, STRIP)
                rows = pl.ds(pl.multiple_of(row + at, STRIP), STRIP)
                for c in range(HALVES):
                    target[lane + c, rows, :] = target[lane + c, rows, :] + step * feed[slot, c, pl.ds(at, STRIP), :]
                return 0

            lax.fori_loop(0, REACH // STRIP, strip, 0, unroll=8)

    out_copies = []

    def send(src, dst):
        copy = pltpu.make_async_copy(src, dst, out_sems.at[len(out_copies)])
        copy.start()
        out_copies.append(copy)

    def middle(tile, count, block):
        e_lane, m_lane = (tile - e_first) * HALVES, (tile - m_first) * HALVES

        def put(c, i, value, rate):
            rows = pl.ds(pl.multiple_of(block * REACH + i * STRIP, STRIP), STRIP)
            mid[m_lane + c, rows, :] = value + (0.5 * DT) * rate

        index = band_tiles.index(tile) * HALVES
        block_rates(win, e_lane, count, (block + 1) * REACH, coef, block * REACH, band, index, put)
        if fed:
            for d in range(count):
                add_source(mid, m_lane + d * HALVES, block * REACH, 0, tile + d, block, 0.5 * DT)

    def end(tile, count, block):
        e_lane, m_lane = (tile - e_first) * HALVES, (tile - m_first) * HALVES

        def put(c, i, value, rate):
            rows = pl.ds(pl.multiple_of((block + 1) * REACH + i * STRIP, STRIP), STRIP)
            win[e_lane + c, rows, :] = win[e_lane + c, rows, :] + DT * rate

        index = band_tiles.index(tile) * HALVES
        block_rates(mid, m_lane, count, block * REACH, coef, block * REACH, band, index, put)
        if fed:
            for d in range(count):
                add_source(win, e_lane + d * HALVES, (block + 1) * REACH, 1, tile + d, block, DT)

    wait(first)
    for tile, count in runs(a_own):
        middle(tile, count, 1)
        middle(tile, count, 2)
    for tile, out in zip(a_own, outs):
        send(mid.at[pair(tile - m_first), mid_rows, :], out)
    wait(second)
    for tile, count in runs(a_near):
        middle(tile, count, 0)
        middle(tile, count, 3)
    wait(third)
    for tile, count in runs(b):
        for block in (1, 2):
            end(tile, count, block)
            for c in range(count * HALVES):
                lane = pl.multiple_of((base + tile) * REACH + c * LANES, LANES)
                rows = pl.ds((block + 1) * REACH, REACH)
                dst = outs[-1].at[pl.ds((block - 1) * REACH, REACH), pl.ds(lane, LANES)]
                send(win.at[(tile - e_first) * HALVES + c, rows, :], dst)
    wait(out_copies)


def run_tiles(key, operands):
    names, a_own, a_near, b, own_loads, near_loads, far_loads, mid_loads, modes, fed, slab_shape = key
    tiles = [t for *_, t in own_loads + near_loads]
    e_first, e_count = min(tiles), max(tiles) - min(tiles) + 1
    tiles = sorted(set(a_own) | set(a_near) | {t + d for t in b for d in (-1, 0, 1)})
    m_first, m_count = tiles[0], tiles[-1] - tiles[0] + 1
    n_band = len(set(a_own) | set(a_near) | set(b))
    plan = key[:8] + (e_first, m_first, modes, slab_shape[1], fed)
    f32 = jnp.float32
    whole = pl.BlockSpec(memory_space=pl.ANY)
    shapes = [jax.ShapeDtypeStruct((HALVES, 2 * REACH, LANES), f32) for _ in a_own]
    if b:
        shapes.append(jax.ShapeDtypeStruct(slab_shape, f32))
    aliases = {names.index("prev"): len(a_own)} if "prev" in names else {}
    n_loads = HALVES * (len(own_loads) + len(near_loads) + len(far_loads)) + len(mid_loads) + n_band + 3
    n_feeds = 2 * (len(a_own) + len(a_near) + len(b)) if fed else 1
    work = 2 * (len(a_own) + len(a_near) + len(b)) * REACH * REACH
    return pl.pallas_call(
        functools.partial(tile_kernel, plan),
        out_shape=shapes,
        in_specs=[pl.BlockSpec(memory_space=pltpu.SMEM) if n == "base" else whole for n in names],
        out_specs=[whole] * len(shapes),
        scratch_shapes=[
            pltpu.VMEM((e_count * HALVES, 6 * REACH, LANES), f32),
            pltpu.VMEM((m_count * HALVES, 4 * REACH, LANES), f32),
            pltpu.VMEM((7, 4 * REACH, LANES), f32),
            pltpu.VMEM((n_band * HALVES, 7, STRIP, LANES), f32),
            pltpu.VMEM((n_feeds, HALVES, REACH, LANES), f32),
            pltpu.SemaphoreType.DMA((n_loads,)),
            pltpu.SemaphoreType.DMA((len(a_own) + 2 * HALVES * len(b),)),
            pltpu.SemaphoreType.DMA((n_feeds,)),
        ],
        input_output_aliases=aliases,
        compiler_params=pltpu.CompilerParams(vmem_limit_bytes=VMEM),
        cost_estimate=pl.CostEstimate(flops=28 * work, bytes_accessed=40 * work, transcendentals=0),
    )(*operands)


RUNS = {}


class Field:
    def __init__(self, slab, coef, band, feed, modes):
        self.slab, self.coef, self.band, self.feed, self.modes = slab, coef, band, feed, modes
        self.tiles = slab.shape[1] // REACH
        self.parts = {}
        self.mids = {}
        self.out = None
        self.last = None

    def step(self, base, a_own, a_near, b):
        operands = {"base": jnp.full((1,), base, jnp.int32)}
        own_loads, near_loads, far_loads, mid_loads = [], [], [], []
        for t in sorted({t + d for t in a_own for d in (-1, 0, 1)} | set(a_near) | set(b)):
            at = base + t
            if at < 0:
                name, value, place, from_base = "left", self.left, at + 2, False
            elif at >= self.tiles:
                name, value, place, from_base = "right", self.right, at - self.tiles, False
            else:
                name, value, place, from_base = "slab", self.slab, t, True
            operands[name] = value
            own_loads.append((name, place, from_base, t))

        def piece(kind, t):
            value, offset = self.parts[kind, base + t]
            name = f"{kind if value.shape[0] == 2 * REACH else kind[0]}{t}"
            operands[name] = value
            return kind, name, offset, t

        for t in sorted(set(a_own) | {t + d for t in a_near for d in (-1, 0, 1)}):
            near_loads += [piece(kind, t) for kind in ("PN", "QN")]
        for t in a_near:
            far_loads += [piece(kind, t) for kind in ("PF", "QF")]
        for t in sorted({t + d for t in b for d in (-1, 0, 1)} - set(a_own)):
            operands[f"M{t}"] = self.mids[base + t]
            mid_loads.append((f"M{t}", t))
        operands["coef"], operands["band"] = self.coef, self.band
        fed = self.feed is not None
        if fed:
            operands["feed"] = self.feed
        if b and self.out is not None:
            operands["prev"] = self.out
        loads = (tuple(own_loads), tuple(near_loads), tuple(far_loads), tuple(mid_loads))
        key = (tuple(operands), tuple(a_own), tuple(a_near), tuple(b)) + loads
        key += (self.modes, fed, self.slab.shape)
        if key not in RUNS:
            RUNS[key] = jax.jit(functools.partial(run_tiles, key))
        results = RUNS[key](tuple(operands.values()))
        for t, value in zip(a_own, results):
            self.mids[base + t] = value
        if b:
            self.out = results[-1]
        self.last = results[0]


def shards(g_start, cotangent, damping, hopping, bonds, source):
    rows_dev, cols_dev = g_start.shape
    modes = damping.shape[0]
    n_row, n_col = lax.axis_size("row"), lax.axis_size("col")
    tiles = cols_dev // REACH
    assert rows_dev == 2 * REACH and cols_dev % REACH == 0 and tiles >= 3 and n_row % 2 == 0
    row_axis = lax.axis_index("row")
    odd = lax.rem(row_axis, 2)
    row_first = row_axis * rows_dev
    col_first = lax.axis_index("col") * cols_dev

    def ring(array, first, count):
        extra = 2 * REACH
        array = jnp.concatenate([array[:, modes - extra :], array, array[:, :extra]], axis=1)
        return lax.dynamic_slice_in_dim(array, first + extra, count, 1)

    def gathered(first, count):
        wide = count + 2 * REACH
        damp = ring(damping[None, :], first - REACH, wide)
        hop = ring(hopping, first - REACH, wide)
        bond = ring(bonds, first - REACH, wide).astype(jnp.float32)
        coef = jnp.concatenate([-damp, hop], axis=0) * bond
        turned = [coef[m, REACH + o : REACH + o + count] for m, o in zip(MIRROR, OFFSETS)]
        return coef[:, REACH : REACH + count], jnp.stack(turned)

    count = 4 * REACH
    inside = row_first - REACH + lax.iota(jnp.int32, count)
    inside = (inside >= 0) & (inside < n_row * rows_dev)
    feed = jnp.where(inside[None, :], ring(source, row_first - REACH, count), 0.0)
    shape = (4, 3, HALVES, REACH, LANES)
    axis = functools.partial(lax.broadcasted_iota, jnp.int32, shape)
    rel = (axis(1) - 1) * REACH + axis(2) * LANES + axis(4) - axis(3)
    dense = jnp.zeros(shape, jnp.float32)
    for k, offset in enumerate(OFFSETS):
        dense = dense + jnp.where(rel == offset, feed[k].reshape(4, 1, 1, REACH, 1), 0.0)
    row_coefs = gathered(row_first - REACH, count)
    col_coefs = gathered(col_first - REACH, cols_dev + 2 * REACH)

    def row_table(coef):
        coef = jnp.where(inside[None, :], coef, 0.0)
        return jnp.broadcast_to(coef[:, :, None], (7, count, LANES))

    def col_table(coef):
        coef = coef.reshape(7, (tiles + 2) * HALVES, 1, LANES).transpose(1, 0, 2, 3)
        return jnp.broadcast_to(coef, ((tiles + 2) * HALVES, 7, STRIP, LANES))

    fields = [
        Field(slab, row_table(row), col_table(col), fed, modes)
        for slab, row, col, fed in zip((g_start, cotangent), row_coefs, col_coefs, (dense, None))
    ]

    swap = [(i, i ^ 1) for i in range(n_row)]
    relay = [(i, i + 2) for i in range(0, n_row - 2, 2)] + [(i, i - 2) for i in range(3, n_row, 2)]
    to_right = [(i, (i + 1) % n_col) for i in range(n_col)]
    to_left = [((i + 1) % n_col, i) for i in range(n_col)]

    swapped, relayed = [], []
    holds = {}

    def after(value, others):
        others = [other for other in others if other is not None]
        if not others:
            return value
        return lax.optimization_barrier((value, *others))[0]

    def exchange(field, tile, halves):
        pieces = []
        for half in halves:
            start = (odd if half == 0 else 1 - odd) * REACH
            for c in range(HALVES):
                at = (start, tile * REACH + c * LANES)
                pieces.append(lax.dynamic_slice(field.slab, at, (REACH, LANES)))
        piece = jnp.concatenate(pieces, axis=0)
        index = len(swapped)
        earlier = swapped[index - IN_FLIGHT] if index >= IN_FLIGHT else None
        got = lax.ppermute(after(piece, [earlier, holds.pop(index, None)]), "row", swap)
        earlier = relayed[index - IN_FLIGHT] if index >= IN_FLIGHT else None
        passed = lax.ppermute(after(got, [earlier]), "row", relay)
        swapped.append(got)
        relayed.append(passed)
        for place, half in enumerate(halves):
            field.parts["PN" if half else "PF", tile] = got, place * HALVES
            field.parts["QF" if half else "QN", tile] = passed, place * HALVES

    def edge(field, source_tile, target_tile, route):
        for kinds in (("PF", "PN"), ("QN", "QF")):
            moved = lax.ppermute(field.parts[kinds[0], source_tile][0], "col", route)
            for place, kind in enumerate(kinds):
                field.parts[kind, target_tile] = moved, place * HALVES

    for field in fields:

        def step(*args, field=field):
            field.step(*args)
            holds[len(swapped) - 1 + HOLD] = field.last

        field.left = lax.ppermute(field.slab[:, cols_dev - 2 * REACH :], "col", to_right)
        field.right = lax.ppermute(field.slab[:, : 2 * REACH], "col", to_left)
        last = tiles - 2
        exchange(field, 0, (0, 1))
        edge(field, 0, tiles, to_left)
        exchange(field, tiles - 1, (0, 1))
        edge(field, tiles - 1, -1, to_right)
        step(0, (-1, 0), (), ())
        for tile in range(1, last):
            exchange(field, tile, (0, 1))
            if tile % 2 == 0:
                step(tile, (-1, 0), (-2, -1), (-2, -1))
            elif tile == last - 1:
                step(tile, (0,), (-1,), (-1,))
        exchange(field, last, (0,))
        exchange(field, last, (1,))
        step(last, (1, 2), (), ())
        step(last, (0,), (-1, 1), (-1, 1))
        step(last, (), (0,), (0,))
    return tuple(field.out for field in fields)


def solution(mesh):
    return jax.shard_map(
        shards,
        mesh=mesh,
        in_specs=(P("row", "col"), P("row", "col"), P(), P(), P(), P()),
        out_specs=(P("row", "col"), P("row", "col")),
        check_vma=False,
    )
```

time: 786 us -> 511 us (0.65); the launches traced: 785 us -> 501 us
  waiting for transfers between devices: 444 us -> 81.1 us
  Pallas kernels: 0 us -> 200 us
  other arithmetic: 221 us -> 27.1 us
  starting transfers between devices: 35 us -> 139 us
  local copies, waits for them, and re-layouts: 84 us -> 49.6 us
    ppermute x16 -> x80, waiting for transfers between devices: 444 us -> 81.1 us  [the longest x34 39.6 us: exchange(): passed = lax.ppermute(after(got, [earlier]), 'row', relay)]
    pallas_call x0 -> x22, Pallas kernels: none -> 200 us  [run_tiles(): pl.pallas_call(functools.partial(tile_kernel, plan), out_shape=shapes, in...]
    add x4 -> x1, other arithmetic: 201 us -> 4.37 us  [shards(): dense + jnp.where(rel == offset, feed[k].reshape(4, 1, 1, REACH, 1), 0.0)]
    ppermute x16 -> x80, starting transfers between devices: 35 us -> 139 us  [the longest x34 97.3 us: exchange(): passed = lax.ppermute(after(got, [earlier]), 'row', relay)]
    slice x28 -> x10, local copies, waits for them, and re-layouts: 36 us -> 8.49 us  [the longest x2 4.52 us: shards(): field.right = lax.ppermute(field.slab[:, :2 * REACH], 'col', to_left)]
    unnamed x20 -> x282, local copies, waits for them, and re-layouts: 37 us -> 25.3 us
    concatenate x4 -> x0, local copies, waits for them, and re-layouts: 11 us -> none  [padded(): jnp.concatenate([lax.ppermute(tail, axis, [(i, (i + 1) % count) for i in...]
    dynamic_slice x0 -> x4, local copies, waits for them, and re-layouts: none -> 10.9 us  [the longest x2 10.9 us: exchange(): pieces.append(lax.dynamic_slice(field.slab, at, (REACH, LANES)))]
  transfers between devices with their start and end apart: 16 -> 80, of which waited for: 7 -> 17; matrix products, arithmetic and copies ran while one was open for 31% -> 9% of each run, Pallas kernels for 0% -> 39%
where the time goes in v1:
time: 511 us; the launch traced here: 501 us
  Pallas kernels  200 us (39%)
  starting transfers between devices  139 us (27%)
  waiting for transfers between devices  81.1 us (16%)
  local copies, waits for them, and re-layouts  49.6 us (10%)
  other arithmetic  27.1 us (5%)
    pallas_call x22, Pallas kernels, run_tiles(): pl.pallas_call(functools.partial(tile_kernel, plan), out_shape=shapes, in...  200 us
    ppermute x34, starting transfers between devices, exchange(): passed = lax.ppermute(after(got, [earlier]), 'row', relay)  97.3 us
    ppermute x34, waiting for transfers between devices, exchange(): passed = lax.ppermute(after(got, [earlier]), 'row', relay)  39.6 us
    ppermute x34, starting transfers between devices, exchange(): lax.ppermute(after(piece, [earlier, holds.pop(index, None)]), 'row', swap)  37.1 us
    ppermute x34, waiting for transfers between devices, exchange(): lax.ppermute(after(piece, [earlier, holds.pop(index, None)]), 'row', swap)  26 us
    unnamed x282, local copies, waits for them, and re-layouts  25.3 us
    ppermute x8, waiting for transfers between devices, edge(): moved = lax.ppermute(field.parts[kinds[0], source_tile][0], 'col', route)  15.6 us
    concatenate x33, other arithmetic, exchange(): piece = jnp.concatenate(pieces, axis=0)  14.7 us
  transfers between devices with their start and end apart: 80, of which 17 were waited for; matrix products, arithmetic and copies ran while one was open for 9% of the time, Pallas kernels for 39%

profile of v1, /device:TPU:0, one launch (start us, length us, event | category | flops | bytes accessed | tf_op | source)
XLA Modules:
  0.0 500.6 jit_solution(17406235003364609603)
XLA Ops:
  0.6 6.6 %constant_dynamic-slice_fusion.13 = (f32[256,128]{1,0:T(8,128)}, f32[256,128]{1,0:T(8,128)}, f32[256,128]{1,0:T(8,128)}, f32[256,128]{1,0:T(8,128)}, f32[256,128...) fusion(f32[512,4096]{1,0:T(8,128)} %refs_1_.44, ...), kind=kLoop, calls=%fused_computation.82 | loop fusion | bytes 16777224 | tf_op jit(solution)/shard_map/dynamic_slice | solution.py:392
  8.1 2.9 collective-permute-start
  11.0 3.0 fusion.14
  30.4 4.4 select_add_fusion.refs_9_.refs_14_.refs_12_.refs_18_.refs_15_
  38.2 3.5 collective-permute-start.6
  41.7 7.0 %collective-permute-done.1.refs_6_.refs_2_ = f32[1024,128]{1,0:T(8,128)} collective-permute-done((f32[1024,128]{1,0:T(8,128)S(1)}, f32[1024,128]{1,0:T(8,128)}, u32[]{:S(2)}, u32[]{:S(2)}) %collective-permute-start.1) | collective-permute-done | bytes 524320 | tf_op jit(solution)/shard_map/ppermute | solution.py:396
  48.7 4.5 collective-permute-start.8
  54.0 11.4 %collective-permute-done.8.refs_6_.refs_5_ = f32[1024,128]{1,0:T(8,128)S(1)} collective-permute-done((f32[1024,128]{1,0:T(8,128)S(1)}, f32[1024,128]{1,0:T(8,128)S(1)}, u32[]{:S(2)}, u32[]{:S(2)}) %collective-permute-start.8) | collective-permute-done | bytes 524320 | tf_op jit(solution)/shard_map/ppermute | solution.py:398
  66.2 2.5 collective-permute-start.2
  68.7 2.7 collective-permute-start.10
  77.8 6.4 %collective-permute-done.7.refs_4_.refs_3_ = f32[1024,128]{1,0:T(8,128)} collective-permute-done((f32[1024,128]{1,0:T(8,128)S(1)}, f32[1024,128]{1,0:T(8,128)}, u32[]{:S(2)}, u32[]{:S(2)}) %collective-permute-start.7) | collective-permute-done | bytes 524320 | tf_op jit(solution)/shard_map/ppermute | solution.py:407
  85.3 3.4 copy-done
  89.8 4.1 run_tiles.12
  99.4 10.2 %run_tiles.13 = (f32[2,512,128]{2,1,0:T(8,128)S(1)}, f32[2,512,128]{2,1,0:T(8,128)S(1)}, f32[512,4096]{1,0:T(8,128)}) custom-call(s32[1]{0:T(128)} %constant.123.clone.1.refs_0_, f32[512,4096]{1,0:T(8,128)S(1)} %copy-done, f32[1024,128]{1,0:T(8,128)S(1)} %copy-done.37, f32[1024,128]{1,0:T(8,128)} %collective-permute-done.7.refs_4_.refs_3_, ...), custom_call_target="tpu_custom_call" | custom-call | flops 22020096 | bytes 31457280 | tf_op jit(solution)/shard_map/jit(run_tiles)/pallas_call | solution.py:242
  111.5 2.9 collective-permute-start.18
  114.6 6.7 %collective-permute-done.16.refs_9_.refs_5_ = f32[1024,128]{1,0:T(8,128)S(1)} collective-permute-done((f32[1024,128]{1,0:T(8,128)S(1)}, f32[1024,128]{1,0:T(8,128)S(1)}, u32[]{:S(2)}, u32[]{:S(2)}) %collective-permute-start.16) | collective-permute-done | bytes 524320 | tf_op jit(solution)/shard_map/ppermute | solution.py:398
  121.3 4.6 collective-permute-start.20
  126.1 10.1 %run_tiles.24 = (f32[2,512,128]{2,1,0:T(8,128)S(1)}, f32[2,512,128]{2,1,0:T(8,128)S(1)}, f32[512,4096]{1,0:T(8,128)}) custom-call(s32[1]{0:T(128)} %constant.39.clone.1.refs_0_, f32[512,4096]{1,0:T(8,128)S(1)} %copy-done, f32[1024,128]{1,0:T(8,128)} %collective-permute-done.1.refs_6_.refs_2_, ...), custom_call_target="tpu_custom_call", output_to_operand_aliasing={{2}: (15, {})} | custom-call | flops 22020096 | bytes 31457280 | tf_op jit(solution)/shard_map/jit(run_tiles)/pallas_call | solution.py:242
  136.2 2.4 collective-permute-start.17
  140.7 3.1 collective-permute-done.20.refs_9_.refs_5_
  143.8 4.4 collective-permute-start.24
  148.4 12.1 %run_tiles.25 = (f32[2,512,128]{2,1,0:T(8,128)S(1)}, f32[2,512,128]{2,1,0:T(8,128)S(1)}, f32[512,4096]{1,0:T(8,128)}) custom-call(s32[1]{0:T(128)} %constant.44.clone.1.refs_0_, f32[512,4096]{1,0:T(8,128)S(1)} %copy-done, f32[1024,128]{1,0:T(8,128)S(1)} %collective-permute-done.2.refs_6_.refs_2_, ...), custom_call_target="tpu_custom_call", output_to_operand_aliasing={{2}: (15, {})} | custom-call | flops 22020096 | bytes 31457280 | tf_op jit(solution)/shard_map/jit(run_tiles)/pallas_call | solution.py:242
  160.5 2.2 collective-permute-start.21
  162.8 2.5 collective-permute-start.26
  166.2 4.4 collective-permute-start.30
  170.8 12.3 %run_tiles.26 = (f32[2,512,128]{2,1,0:T(8,128)S(1)}, f32[2,512,128]{2,1,0:T(8,128)S(1)}, f32[512,4096]{1,0:T(8,128)}) custom-call(s32[1]{0:T(128)} %constant.48.clone.1.refs_0_, f32[512,4096]{1,0:T(8,128)S(1)} %copy-done, f32[1024,128]{1,0:T(8,128)S(1)} %collective-permute-done.9.refs_6_.refs_2_, ...), custom_call_target="tpu_custom_call", output_to_operand_aliasing={{2}: (15, {})} | custom-call | flops 22020096 | bytes 31457280 | tf_op jit(solution)/shard_map/jit(run_tiles)/pallas_call | solution.py:242
  185.1 2.7 collective-permute-start.27
  189.4 4.7 collective-permute-start.34
  194.1 12.1 %run_tiles.27 = (f32[2,512,128]{2,1,0:T(8,128)S(1)}, f32[2,512,128]{2,1,0:T(8,128)S(1)}, f32[512,4096]{1,0:T(8,128)}) custom-call(s32[1]{0:T(128)} %constant.55.clone.1.refs_0_, f32[512,4096]{1,0:T(8,128)S(1)} %copy-done, f32[1024,128]{1,0:T(8,128)S(1)} %collective-permute-done.13.refs_6_.refs_2_, ...), custom_call_target="tpu_custom_call", output_to_operand_aliasing={{2}: (15, {})} | custom-call | flops 22020096 | bytes 31457280 | tf_op jit(solution)/shard_map/jit(run_tiles)/pallas_call | solution.py:242
  210.7 4.3 constant_dynamic-slice_fusion.11
  228.6 11.7 %run_tiles.28 = (f32[2,512,128]{2,1,0:T(8,128)S(1)}, f32[2,512,128]{2,1,0:T(8,128)S(1)}, f32[512,4096]{1,0:T(8,128)}) custom-call(s32[1]{0:T(128)} %constant.21.clone.1.refs_0_, f32[512,4096]{1,0:T(8,128)S(1)} %bitcast.8, f32[1024,128]{1,0:T(8,128)S(1)} %copy-done.13, f32[1024,128]{1,0:T(8,128)S(1)} %copy-done.17, ...), custom_call_target="tpu_custom_call", output_to_operand_aliasing={{2}: (15, {})} | custom-call | flops 22020096 | bytes 31457280 | tf_op jit(solution)/shard_map/jit(run_tiles)/pallas_call | solution.py:242
  242.3 2.5 collective-permute-start.35
  248.1 3.8 collective-permute-done.35.refs_7_.refs_5_
  252.1 6.9 %run_tiles.14 = (f32[2,512,128]{2,1,0:T(8,128)S(1)}, f32[512,4096]{1,0:T(8,128)}) custom-call(s32[1]{0:T(128)} %constant.140.clone.1.refs_0_, f32[512,4096]{1,0:T(8,128)S(1)} %bitcast.8, f32[1024,128]{1,0:T(8,128)S(1)} %copy-done.11, f32[1024,128]{1,0:T(8,128)S(1)} %copy-done.20, ...), custom_call_target="tpu_custom_call", output_to_operand_aliasing={{1}: (13, {})} | custom-call | flops 11010048 | bytes 15728640 | tf_op jit(solution)/shard_map/jit(run_tiles)/pallas_call | solution.py:242
  261.8 2.2 collective-permute-start.48
  268.6 4.9 collective-permute-done.41.refs_6_.refs_2_
  277.4 4.0 run_tiles.15
  281.4 11.0 %run_tiles.16 = (f32[2,512,128]{2,1,0:T(8,128)S(1)}, f32[512,4096]{1,0:T(8,128)}) custom-call(s32[1]{0:T(128)} %constant.27.clone.1.refs_0_, f32[512,4096]{1,0:T(8,128)S(1)} %bitcast.8, f32[1024,128]{1,0:T(8,128)S(1)} %collective-permute-done.32.refs_4_.refs_2_.refs_8_, ...), custom_call_target="tpu_custom_call", output_to_operand_aliasing={{1}: (19, {})} | custom-call | flops 18350080 | bytes 26214400 | tf_op jit(solution)/shard_map/jit(run_tiles)/pallas_call | solution.py:242
  292.4 5.6 %run_tiles.17 = f32[512,4096]{1,0:T(8,128)} custom-call(s32[1]{0:T(128)} %constant.27.clone.1.refs_0_, f32[512,4096]{1,0:T(8,128)S(1)} %bitcast.8, f32[1024,128]{1,0:T(8,128)S(1)} %collective-permute-done.25.refs_6_.refs_4_.refs_2_, f32[1024,128]{1,0:T(8,128)} %collective-permute-done.28.refs_7_.refs_5_.refs_3_, ...), custom_call_target="tpu_custom_call", output_to_operand_aliasing={{}: (16, {})} | custom-call | flops 7340032 | bytes 10485760 | tf_op jit(solution)/shard_map/jit(run_tiles)/pallas_call | solution.py:242
  300.6 2.5 collective-permute-start.50
  308.1 8.8 %collective-permute-done.47.refs_4_.refs_3_ = f32[1024,128]{1,0:T(8,128)S(1)} collective-permute-done((f32[1024,128]{1,0:T(8,128)}, f32[1024,128]{1,0:T(8,128)S(1)}, u32[]{:S(2)}, u32[]{:S(2)}) %collective-permute-start.47) | collective-permute-done | bytes 524320 | tf_op jit(solution)/shard_map/ppermute | solution.py:407
  318.0 3.4 copy-done.1
  321.4 4.0 run_tiles.18
  330.9 10.6 %run_tiles.19 = (f32[2,512,128]{2,1,0:T(8,128)S(1)}, f32[2,512,128]{2,1,0:T(8,128)S(1)}, f32[512,4096]{1,0:T(8,128)}) custom-call(s32[1]{0:T(128)} %constant.123.clone.1.refs_0_, f32[512,4096]{1,0:T(8,128)S(1)} %copy-done.1, f32[1024,128]{1,0:T(8,128)S(1)} %copy-done.34, f32[1024,128]{1,0:T(8,128)S(1)} %collective-permute-done.47.refs_4_.refs_3_, ...), custom_call_target="tpu_custom_call" | custom-call | flops 22020096 | bytes 31457280 | tf_op jit(solution)/shard_map/jit(run_tiles)/pallas_call | solution.py:242
  343.6 2.4 collective-permute-start.58
  346.1 6.7 %collective-permute-done.56.refs_9_.refs_5_ = f32[1024,128]{1,0:T(8,128)S(1)} collective-permute-done((f32[1024,128]{1,0:T(8,128)S(1)}, f32[1024,128]{1,0:T(8,128)S(1)}, u32[]{:S(2)}, u32[]{:S(2)}) %collective-permute-start.56) | collective-permute-done | bytes 524320 | tf_op jit(solution)/shard_map/ppermute | solution.py:398
  352.8 4.8 collective-permute-start.60
  357.9 10.6 %run_tiles.29 = (f32[2,512,128]{2,1,0:T(8,128)S(1)}, f32[2,512,128]{2,1,0:T(8,128)S(1)}, f32[512,4096]{1,0:T(8,128)}) custom-call(s32[1]{0:T(128)} %constant.39.clone.1.refs_0_, f32[512,4096]{1,0:T(8,128)S(1)} %copy-done.1, f32[1024,128]{1,0:T(8,128)} %collective-permute-done.41.refs_6_.refs_2_, ...), custom_call_target="tpu_custom_call", output_to_operand_aliasing={{2}: (14, {})} | custom-call | flops 22020096 | bytes 31457280 | tf_op jit(solution)/shard_map/jit(run_tiles)/pallas_call | solution.py:242
  372.9 2.4 collective-permute-done.60.refs_9_.refs_5_
  375.3 4.4 collective-permute-start.64
  380.0 11.7 %run_tiles.30 = (f32[2,512,128]{2,1,0:T(8,128)S(1)}, f32[2,512,128]{2,1,0:T(8,128)S(1)}, f32[512,4096]{1,0:T(8,128)}) custom-call(s32[1]{0:T(128)} %constant.44.clone.1.refs_0_, f32[512,4096]{1,0:T(8,128)S(1)} %copy-done.1, f32[1024,128]{1,0:T(8,128)S(1)} %collective-permute-done.42.refs_6_.refs_2_, ...), custom_call_target="tpu_custom_call", output_to_operand_aliasing={{2}: (14, {})} | custom-call | flops 22020096 | bytes 31457280 | tf_op jit(solution)/shard_map/jit(run_tiles)/pallas_call | solution.py:242
  397.8 4.4 collective-permute-start.70
  402.4 11.7 %run_tiles.31 = (f32[2,512,128]{2,1,0:T(8,128)S(1)}, f32[2,512,128]{2,1,0:T(8,128)S(1)}, f32[512,4096]{1,0:T(8,128)}) custom-call(s32[1]{0:T(128)} %constant.48.clone.1.refs_0_, f32[512,4096]{1,0:T(8,128)S(1)} %copy-done.1, f32[1024,128]{1,0:T(8,128)S(1)} %collective-permute-done.49.refs_6_.refs_2_, ...), custom_call_target="tpu_custom_call", output_to_operand_aliasing={{2}: (14, {})} | custom-call | flops 22020096 | bytes 31457280 | tf_op jit(solution)/shard_map/jit(run_tiles)/pallas_call | solution.py:242
  420.2 4.6 collective-permute-start.74
  425.0 5.3 %collective-permute-done.65.refs_6_.refs_4_.refs_2_ = f32[1024,128]{1,0:T(8,128)S(1)} collective-permute-done((f32[1024,128]{1,0:T(8,128)S(1)}, f32[1024,128]{1,0:T(8,128)S(1)}, u32[]{:S(2)}, u32[]{:S(2)}) %collective-permute-start.65) | collective-permute-done | bytes 524320 | tf_op jit(solution)/shard_map/ppermute | solution.py:396
  431.5 4.4 collective-permute-start.68
  436.1 11.7 %run_tiles.32 = (f32[2,512,128]{2,1,0:T(8,128)S(1)}, f32[2,512,128]{2,1,0:T(8,128)S(1)}, f32[512,4096]{1,0:T(8,128)}) custom-call(s32[1]{0:T(128)} %constant.55.clone.1.refs_0_, f32[512,4096]{1,0:T(8,128)S(1)} %copy-done.1, f32[1024,128]{1,0:T(8,128)S(1)} %collective-permute-done.53.refs_6_.refs_2_, ...), custom_call_target="tpu_custom_call", output_to_operand_aliasing={{2}: (14, {})} | custom-call | flops 22020096 | bytes 31457280 | tf_op jit(solution)/shard_map/jit(run_tiles)/pallas_call | solution.py:242
  447.9 8.6 %collective-permute-done.71.refs_6_.refs_4_ = f32[512,128]{1,0:T(8,128)S(1)} collective-permute-done((f32[512,128]{1,0:T(8,128)S(1)}, f32[512,128]{1,0:T(8,128)S(1)}, u32[]{:S(2)}, u32[]{:S(2)}) %collective-permute-start.71) | collective-permute-done | bytes 262176 | tf_op jit(solution)/shard_map/ppermute | solution.py:396
  456.6 2.5 collective-permute-start.75
  460.4 4.0 run_tiles.21
  464.4 11.7 %run_tiles.33 = (f32[2,512,128]{2,1,0:T(8,128)S(1)}, f32[2,512,128]{2,1,0:T(8,128)S(1)}, f32[512,4096]{1,0:T(8,128)}) custom-call(s32[1]{0:T(128)} %constant.21.clone.1.refs_0_, f32[512,4096]{1,0:T(8,128)S(1)} %copy-done.1, f32[1024,128]{1,0:T(8,128)S(1)} %collective-permute-done.57.refs_6_.refs_2_, ...), custom_call_target="tpu_custom_call", output_to_operand_aliasing={{2}: (14, {})} | custom-call | flops 22020096 | bytes 31457280 | tf_op jit(solution)/shard_map/jit(run_tiles)/pallas_call | solution.py:242
  476.1 7.2 %run_tiles.20 = (f32[2,512,128]{2,1,0:T(8,128)S(1)}, f32[512,4096]{1,0:T(8,128)}) custom-call(s32[1]{0:T(128)} %constant.140.clone.1.refs_0_, f32[512,4096]{1,0:T(8,128)S(1)} %copy-done.1, f32[1024,128]{1,0:T(8,128)S(1)} %collective-permute-done.61.refs_2_.refs_6_, ...), custom_call_target="tpu_custom_call", output_to_operand_aliasing={{1}: (12, {})} | custom-call | flops 11010048 | bytes 15728640 | tf_op jit(solution)/shard_map/jit(run_tiles)/pallas_call | solution.py:242
  483.3 11.2 %run_tiles.22 = (f32[2,512,128]{2,1,0:T(8,128)S(1)}, f32[512,4096]{1,0:T(8,128)}) custom-call(s32[1]{0:T(128)} %constant.27.clone.1.refs_0_, f32[512,4096]{1,0:T(8,128)S(1)} %copy-done.1, f32[1024,128]{1,0:T(8,128)S(1)} %collective-permute-done.72.refs_4_.refs_2_.refs_8_, ...), custom_call_target="tpu_custom_call", output_to_operand_aliasing={{1}: (18, {})} | custom-call | flops 18350080 | bytes 26214400 | tf_op jit(solution)/shard_map/jit(run_tiles)/pallas_call | solution.py:242
  494.5 5.8 %run_tiles.23 = f32[512,4096]{1,0:T(8,128)} custom-call(s32[1]{0:T(128)} %constant.27.clone.1.refs_0_, f32[512,4096]{1,0:T(8,128)S(1)} %copy-done.1, f32[1024,128]{1,0:T(8,128)S(1)} %collective-permute-done.65.refs_6_.refs_4_.refs_2_, f32[1024,128]{1,0:T(8,128)S(1)} %collective-permute-done.68.refs_7_.refs_5_.refs_3_, ...), custom_call_target="tpu_custom_call", output_to_operand_aliasing={{}: (15, {})} | custom-call | flops 7340032 | bytes 10485760 | tf_op jit(solution)/shard_map/jit(run_tiles)/pallas_call | solution.py:242
  (478 shorter events, 114.8 us)
Async XLA Ops:
  8.1 26.7 %collective-permute-start = (f32[1024,128]{1,0:T(8,128)}, f32[1024,128]{1,0:T(8,128)S(1)}, u32[]{:S(2)}, u32[]{:S(2)}) collective-permute-start(f32[1024,128]{1,0:T(8,128)} %pad_maximum_fusion.8), channel_id=1, source_target_pairs={{0,8},{8,0},{16,24},{24,16},{1,9},{9,1},{17,25},{25,17},{2,10},{10... | collective-permute-start | bytes 1572872 | tf_op jit(solution)/shard_map/ppermute | solution.py:396
  14.0 59.5 %collective-permute-start.3 = (f32[512,512]{1,0:T(8,128)}, f32[512,512]{1,0:T(8,128)}, u32[]{:S(2)}, u32[]{:S(2)}) collective-permute-start(f32[512,512]{1,0:T(8,128)} %get-tuple-element.308), channel_id=1, source_target_pairs={{0,1},{1,2},{2,3},{3,4},{4,5},{5,6},{6,7},{7,0},{8,9},{9,10},{10,1... | collective-permute-start | bytes 3145736 | tf_op jit(solution)/shard_map/ppermute | solution.py:417
  14.8 21.9 %collective-permute-start.4 = (f32[1024,128]{1,0:T(8,128)}, f32[1024,128]{1,0:T(8,128)S(1)}, u32[]{:S(2)}, u32[]{:S(2)}) collective-permute-start(f32[1024,128]{1,0:T(8,128)} %pad_maximum_fusion.9), channel_id=1, source_target_pairs={{0,8},{8,0},{16,24},{24,16},{1,9},{9,1},{17,25},{25,17},{2,10},{10... | collective-permute-start | bytes 1572872 | tf_op jit(solution)/shard_map/ppermute | solution.py:396
  36.8 34.6 %collective-permute-start.11 = (f32[1024,128]{1,0:T(8,128)S(1)}, f32[1024,128]{1,0:T(8,128)}, u32[]{:S(2)}, u32[]{:S(2)}) collective-permute-start(f32[1024,128]{1,0:T(8,128)S(1)} %get-tuple-element.123), channel_id=1, source_target_pairs={{0,8},{8,0},{16,24},{24,16},{1,9},{9,1},{17,25},{25,17},{2,10},{10... | collective-permute-start | bytes 1572872 | tf_op jit(solution)/shard_map/ppermute | solution.py:396
  36.9 36.7 %collective-permute-start.5 = (f32[1024,128]{1,0:T(8,128)S(1)}, f32[1024,128]{1,0:T(8,128)S(1)}, u32[]{:S(2)}, u32[]{:S(2)}) collective-permute-start(f32[1024,128]{1,0:T(8,128)S(1)} %collective-permute-done.4.refs_3_.refs_8_.refs_6_), channel_id=1, source_target_pairs={{0,1},{1,2},{2,3},{3,4},{4,5},{5,6},{6,7},{7,0},{8,9},{9,10},{10,1... | collective-permute-start | bytes 1572872 | tf_op jit(solution)/shard_map/ppermute | solution.py:407
  38.2 30.5 %collective-permute-start.6 = (f32[1024,128]{1,0:T(8,128)S(1)}, f32[1024,128]{1,0:T(8,128)S(1)}, u32[]{:S(2)}, u32[]{:S(2)}) collective-permute-start(f32[1024,128]{1,0:T(8,128)S(1)} %collective-permute-done.4.refs_3_.refs_8_.refs_6_), channel_id=1, source_target_pairs={{0,16},{24,8},{1,17},{25,9},{2,18},{26,10},{3,19},{27,11},{4,20},{... | collective-permute-start | bytes 1572872 | tf_op jit(solution)/shard_map/ppermute | solution.py:398
  48.7 16.7 %collective-permute-start.8 = (f32[1024,128]{1,0:T(8,128)S(1)}, f32[1024,128]{1,0:T(8,128)S(1)}, u32[]{:S(2)}, u32[]{:S(2)}) collective-permute-start(f32[1024,128]{1,0:T(8,128)S(1)} %collective-permute-done.refs_5_.refs_4_), channel_id=1, source_target_pairs={{0,16},{24,8},{1,17},{25,9},{2,18},{26,10},{3,19},{27,11},{4,20},{... | collective-permute-start | bytes 1572872 | tf_op jit(solution)/shard_map/ppermute | solution.py:398
  66.2 27.6 %collective-permute-start.2 = (f32[1024,128]{1,0:T(8,128)}, f32[1024,128]{1,0:T(8,128)S(1)}, u32[]{:S(2)}, u32[]{:S(2)}) collective-permute-start(f32[1024,128]{1,0:T(8,128)} %pad_maximum_fusion.6), channel_id=1, source_target_pairs={{0,8},{8,0},{16,24},{24,16},{1,9},{9,1},{17,25},{25,17},{2,10},{10... | collective-permute-start | bytes 1572872 | tf_op jit(solution)/shard_map/ppermute | solution.py:396
  68.7 27.1 %collective-permute-start.10 = (f32[1024,128]{1,0:T(8,128)}, f32[1024,128]{1,0:T(8,128)}, u32[]{:S(2)}, u32[]{:S(2)}) collective-permute-start(f32[1024,128]{1,0:T(8,128)} %collective-permute-done.1.refs_6_.refs_2_), channel_id=1, source_target_pairs={{0,16},{24,8},{1,17},{25,9},{2,18},{26,10},{3,19},{27,11},{4,20},{... | collective-permute-start | bytes 1572872 | tf_op jit(solution)/shard_map/ppermute | solution.py:398
  71.5 26.4 %collective-permute-start.12 = (f32[1024,128]{1,0:T(8,128)}, f32[1024,128]{1,0:T(8,128)}, u32[]{:S(2)}, u32[]{:S(2)}) collective-permute-start(f32[1024,128]{1,0:T(8,128)} %collective-permute-done.11.refs_8_.refs_4_), channel_id=1, source_target_pairs={{0,16},{24,8},{1,17},{25,9},{2,18},{26,10},{3,19},{27,11},{4,20},{... | collective-permute-start | bytes 1572872 | tf_op jit(solution)/shard_map/ppermute | solution.py:398
  73.5 24.3 %collective-permute-start.15 = (f32[1024,128]{1,0:T(8,128)}, f32[1024,128]{1,0:T(8,128)S(1)}, u32[]{:S(2)}, u32[]{:S(2)}) collective-permute-start(f32[1024,128]{1,0:T(8,128)} %pad_maximum_fusion.11), channel_id=1, source_target_pairs={{0,8},{8,0},{16,24},{24,16},{1,9},{9,1},{17,25},{25,17},{2,10},{10... | collective-permute-start | bytes 1572872 | tf_op jit(solution)/shard_map/ppermute | solution.py:396
  97.8 23.5 %collective-permute-start.16 = (f32[1024,128]{1,0:T(8,128)S(1)}, f32[1024,128]{1,0:T(8,128)S(1)}, u32[]{:S(2)}, u32[]{:S(2)}) collective-permute-start(f32[1024,128]{1,0:T(8,128)S(1)} %collective-permute-done.15.refs_8_.refs_4_), channel_id=1, source_target_pairs={{0,16},{24,8},{1,17},{25,9},{2,18},{26,10},{3,19},{27,11},{4,20},{... | collective-permute-start | bytes 1572872 | tf_op jit(solution)/shard_map/ppermute | solution.py:398
  99.2 22.1 %collective-permute-start.19 = (f32[1024,128]{1,0:T(8,128)S(1)}, f32[1024,128]{1,0:T(8,128)S(1)}, u32[]{:S(2)}, u32[]{:S(2)}) collective-permute-start(f32[1024,128]{1,0:T(8,128)S(1)} %pad_maximum_fusion.12), channel_id=1, source_target_pairs={{0,8},{8,0},{16,24},{24,16},{1,9},{9,1},{17,25},{25,17},{2,10},{10... | collective-permute-start | bytes 1572872 | tf_op jit(solution)/shard_map/ppermute | solution.py:396
  109.6 26.6 %collective-permute-start.13 = (f32[1024,128]{1,0:T(8,128)S(1)}, f32[1024,128]{1,0:T(8,128)S(1)}, u32[]{:S(2)}, u32[]{:S(2)}) collective-permute-start(f32[1024,128]{1,0:T(8,128)S(1)} %pad_maximum_fusion.4), channel_id=1, source_target_pairs={{0,8},{8,0},{16,24},{24,16},{1,9},{9,1},{17,25},{25,17},{2,10},{10... | collective-permute-start | bytes 1572872 | tf_op jit(solution)/shard_map/ppermute | solution.py:396
  111.5 27.2 %collective-permute-start.18 = (f32[1024,128]{1,0:T(8,128)S(1)}, f32[1024,128]{1,0:T(8,128)S(1)}, u32[]{:S(2)}, u32[]{:S(2)}) collective-permute-start(f32[1024,128]{1,0:T(8,128)S(1)} %collective-permute-done.9.refs_6_.refs_2_), channel_id=1, source_target_pairs={{0,16},{24,8},{1,17},{25,9},{2,18},{26,10},{3,19},{27,11},{4,20},{... | collective-permute-start | bytes 1572872 | tf_op jit(solution)/shard_map/ppermute | solution.py:398
  121.3 22.5 %collective-permute-start.20 = (f32[1024,128]{1,0:T(8,128)S(1)}, f32[1024,128]{1,0:T(8,128)S(1)}, u32[]{:S(2)}, u32[]{:S(2)}) collective-permute-start(f32[1024,128]{1,0:T(8,128)S(1)} %collective-permute-done.19.refs_8_.refs_4_), channel_id=1, source_target_pairs={{0,16},{24,8},{1,17},{25,9},{2,18},{26,10},{3,19},{27,11},{4,20},{... | collective-permute-start | bytes 1572872 | tf_op jit(solution)/shard_map/ppermute | solution.py:398
  125.9 17.9 %collective-permute-start.23 = (f32[1024,128]{1,0:T(8,128)S(1)}, f32[1024,128]{1,0:T(8,128)S(1)}, u32[]{:S(2)}, u32[]{:S(2)}) collective-permute-start(f32[1024,128]{1,0:T(8,128)S(1)} %pad_maximum_fusion.13), channel_id=1, source_target_pairs={{0,8},{8,0},{16,24},{24,16},{1,9},{9,1},{17,25},{25,17},{2,10},{10... | collective-permute-start | bytes 1572872 | tf_op jit(solution)/shard_map/ppermute | solution.py:396
  136.2 24.3 %collective-permute-start.17 = (f32[1024,128]{1,0:T(8,128)S(1)}, f32[1024,128]{1,0:T(8,128)S(1)}, u32[]{:S(2)}, u32[]{:S(2)}) collective-permute-start(f32[1024,128]{1,0:T(8,128)S(1)} %pad_maximum_fusion.3), channel_id=1, source_target_pairs={{0,8},{8,0},{16,24},{24,16},{1,9},{9,1},{17,25},{25,17},{2,10},{10... | collective-permute-start | bytes 1572872 | tf_op jit(solution)/shard_map/ppermute | solution.py:396
  138.7 24.1 %collective-permute-start.22 = (f32[1024,128]{1,0:T(8,128)S(1)}, f32[1024,128]{1,0:T(8,128)S(1)}, u32[]{:S(2)}, u32[]{:S(2)}) collective-permute-start(f32[1024,128]{1,0:T(8,128)S(1)} %collective-permute-done.13.refs_6_.refs_2_), channel_id=1, source_target_pairs={{0,16},{24,8},{1,17},{25,9},{2,18},{26,10},{3,19},{27,11},{4,20},{... | collective-permute-start | bytes 1572872 | tf_op jit(solution)/shard_map/ppermute | solution.py:398
  143.8 22.5 %collective-permute-start.24 = (f32[1024,128]{1,0:T(8,128)S(1)}, f32[1024,128]{1,0:T(8,128)S(1)}, u32[]{:S(2)}, u32[]{:S(2)}) collective-permute-start(f32[1024,128]{1,0:T(8,128)S(1)} %collective-permute-done.23.refs_8_.refs_4_), channel_id=1, source_target_pairs={{0,16},{24,8},{1,17},{25,9},{2,18},{26,10},{3,19},{27,11},{4,20},{... | collective-permute-start | bytes 1572872 | tf_op jit(solution)/shard_map/ppermute | solution.py:398
  148.2 18.1 %collective-permute-start.29 = (f32[1024,128]{1,0:T(8,128)S(1)}, f32[1024,128]{1,0:T(8,128)S(1)}, u32[]{:S(2)}, u32[]{:S(2)}) collective-permute-start(f32[1024,128]{1,0:T(8,128)S(1)} %pad_maximum_fusion.14), channel_id=1, source_target_pairs={{0,8},{8,0},{16,24},{24,16},{1,9},{9,1},{17,25},{25,17},{2,10},{10... | collective-permute-start | bytes 1572872 | tf_op jit(solution)/shard_map/ppermute | solution.py:396
  160.5 22.5 %collective-permute-start.21 = (f32[1024,128]{1,0:T(8,128)S(1)}, f32[1024,128]{1,0:T(8,128)S(1)}, u32[]{:S(2)}, u32[]{:S(2)}) collective-permute-start(f32[1024,128]{1,0:T(8,128)S(1)} %pad_maximum_fusion.2), channel_id=1, source_target_pairs={{0,8},{8,0},{16,24},{24,16},{1,9},{9,1},{17,25},{25,17},{2,10},{10... | collective-permute-start | bytes 1572872 | tf_op jit(solution)/shard_map/ppermute | solution.py:396
  162.8 22.4 %collective-permute-start.26 = (f32[1024,128]{1,0:T(8,128)S(1)}, f32[1024,128]{1,0:T(8,128)S(1)}, u32[]{:S(2)}, u32[]{:S(2)}) collective-permute-start(f32[1024,128]{1,0:T(8,128)S(1)} %collective-permute-done.17.refs_6_.refs_2_), channel_id=1, source_target_pairs={{0,16},{24,8},{1,17},{25,9},{2,18},{26,10},{3,19},{27,11},{4,20},{... | collective-permute-start | bytes 1572872 | tf_op jit(solution)/shard_map/ppermute | solution.py:398
  166.2 23.1 %collective-permute-start.30 = (f32[1024,128]{1,0:T(8,128)S(1)}, f32[1024,128]{1,0:T(8,128)S(1)}, u32[]{:S(2)}, u32[]{:S(2)}) collective-permute-start(f32[1024,128]{1,0:T(8,128)S(1)} %collective-permute-done.29.refs_8_.refs_4_), channel_id=1, source_target_pairs={{0,16},{24,8},{1,17},{25,9},{2,18},{26,10},{3,19},{27,11},{4,20},{... | collective-permute-start | bytes 1572872 | tf_op jit(solution)/shard_map/ppermute | solution.py:398
  170.7 18.7 %collective-permute-start.32 = (f32[1024,128]{1,0:T(8,128)S(1)}, f32[1024,128]{1,0:T(8,128)S(1)}, u32[]{:S(2)}, u32[]{:S(2)}) collective-permute-start(f32[1024,128]{1,0:T(8,128)S(1)} %pad_maximum_fusion.15), channel_id=1, source_target_pairs={{0,8},{8,0},{16,24},{24,16},{1,9},{9,1},{17,25},{25,17},{2,10},{10... | collective-permute-start | bytes 1572872 | tf_op jit(solution)/shard_map/ppermute | solution.py:396
  183.1 24.7 %collective-permute-start.25 = (f32[1024,128]{1,0:T(8,128)S(1)}, f32[1024,128]{1,0:T(8,128)S(1)}, u32[]{:S(2)}, u32[]{:S(2)}) collective-permute-start(f32[1024,128]{1,0:T(8,128)S(1)} %pad_maximum_fusion.1), channel_id=1, source_target_pairs={{0,8},{8,0},{16,24},{24,16},{1,9},{9,1},{17,25},{25,17},{2,10},{10... | collective-permute-start | bytes 1572872 | tf_op jit(solution)/shard_map/ppermute | solution.py:396
  185.1 22.7 %collective-permute-start.27 = (f32[1024,128]{1,0:T(8,128)S(1)}, f32[1024,128]{1,0:T(8,128)S(1)}, u32[]{:S(2)}, u32[]{:S(2)}) collective-permute-start(f32[1024,128]{1,0:T(8,128)S(1)} %collective-permute-done.21.refs_2_.refs_6_), channel_id=1, source_target_pairs={{0,16},{24,8},{1,17},{25,9},{2,18},{26,10},{3,19},{27,11},{4,20},{... | collective-permute-start | bytes 1572872 | tf_op jit(solution)/shard_map/ppermute | solution.py:398
  187.8 76.2 %collective-permute-start.39 = (f32[512,512]{1,0:T(8,128)}, f32[512,512]{1,0:T(8,128)}, u32[]{:S(2)}, u32[]{:S(2)}) collective-permute-start(f32[512,512]{1,0:T(8,128)} %get-tuple-element.307), channel_id=1, source_target_pairs={{1,0},{2,1},{3,2},{4,3},{5,4},{6,5},{7,6},{0,7},{9,8},{10,9},{11,1... | collective-permute-start | bytes 3145736 | tf_op jit(solution)/shard_map/ppermute | solution.py:418
  189.4 28.7 %collective-permute-start.33 = (f32[512,128]{1,0:T(8,128)}, f32[512,128]{1,0:T(8,128)}, u32[]{:S(2)}, u32[]{:S(2)}) collective-permute-start(f32[512,128]{1,0:T(8,128)} %pad_maximum_fusion.32), channel_id=1, source_target_pairs={{0,8},{8,0},{16,24},{24,16},{1,9},{9,1},{17,25},{25,17},{2,10},{10... | collective-permute-start | bytes 786440 | tf_op jit(solution)/shard_map/ppermute | solution.py:396
  189.4 28.9 %collective-permute-start.34 = (f32[1024,128]{1,0:T(8,128)S(1)}, f32[1024,128]{1,0:T(8,128)}, u32[]{:S(2)}, u32[]{:S(2)}) collective-permute-start(f32[1024,128]{1,0:T(8,128)S(1)} %collective-permute-done.32.refs_4_.refs_2_.refs_8_), channel_id=1, source_target_pairs={{0,16},{24,8},{1,17},{25,9},{2,18},{26,10},{3,19},{27,11},{4,20},{... | collective-permute-start | bytes 1572872 | tf_op jit(solution)/shard_map/ppermute | solution.py:398
  208.6 36.3 %collective-permute-start.28 = (f32[1024,128]{1,0:T(8,128)S(1)}, f32[1024,128]{1,0:T(8,128)}, u32[]{:S(2)}, u32[]{:S(2)}) collective-permute-start(f32[1024,128]{1,0:T(8,128)S(1)} %collective-permute-done.25.refs_6_.refs_4_.refs_2_), channel_id=1, source_target_pairs={{0,16},{24,8},{1,17},{25,9},{2,18},{26,10},{3,19},{27,11},{4,20},{... | collective-permute-start | bytes 1572872 | tf_op jit(solution)/shard_map/ppermute | solution.py:398
  210.7 29.7 %collective-permute-start.31 = (f32[512,128]{1,0:T(8,128)}, f32[512,128]{1,0:T(8,128)}, u32[]{:S(2)}, u32[]{:S(2)}) collective-permute-start(f32[512,128]{1,0:T(8,128)} %pad_maximum_fusion.31), channel_id=1, source_target_pairs={{0,8},{8,0},{16,24},{24,16},{1,9},{9,1},{17,25},{25,17},{2,10},{10... | collective-permute-start | bytes 786440 | tf_op jit(solution)/shard_map/ppermute | solution.py:396
  218.0 33.8 %collective-permute-start.40 = (f32[1024,128]{1,0:T(8,128)S(1)}, f32[1024,128]{1,0:T(8,128)S(1)}, u32[]{:S(2)}, u32[]{:S(2)}) collective-permute-start(f32[1024,128]{1,0:T(8,128)S(1)} %pad_maximum_fusion.23), channel_id=1, source_target_pairs={{0,8},{8,0},{16,24},{24,16},{1,9},{9,1},{17,25},{25,17},{2,10},{10... | collective-permute-start | bytes 1572872 | tf_op jit(solution)/shard_map/ppermute | solution.py:396
  240.4 19.2 %collective-permute-start.44 = (f32[1024,128]{1,0:T(8,128)S(1)}, f32[1024,128]{1,0:T(8,128)S(1)}, u32[]{:S(2)}, u32[]{:S(2)}) collective-permute-start(f32[1024,128]{1,0:T(8,128)S(1)} %pad_maximum_fusion.24), channel_id=1, source_target_pairs={{0,8},{8,0},{16,24},{24,16},{1,9},{9,1},{17,25},{25,17},{2,10},{10... | collective-permute-start | bytes 1572872 | tf_op jit(solution)/shard_map/ppermute | solution.py:396
  259.0 45.5 %collective-permute-start.43 = (f32[512,512]{1,0:T(8,128)}, f32[512,512]{1,0:T(8,128)S(1)}, u32[]{:S(2)}, u32[]{:S(2)}) collective-permute-start(f32[512,512]{1,0:T(8,128)} %get-tuple-element.242), channel_id=1, source_target_pairs={{0,1},{1,2},{2,3},{3,4},{4,5},{5,6},{6,7},{7,0},{8,9},{9,10},{10,1... | collective-permute-start | bytes 3145736 | tf_op jit(solution)/shard_map/ppermute | solution.py:417
  261.8 36.3 %collective-permute-start.48 = (f32[1024,128]{1,0:T(8,128)S(1)}, f32[1024,128]{1,0:T(8,128)S(1)}, u32[]{:S(2)}, u32[]{:S(2)}) collective-permute-start(f32[1024,128]{1,0:T(8,128)S(1)} %collective-permute-done.40.refs_5_.refs_4_), channel_id=1, source_target_pairs={{0,16},{24,8},{1,17},{25,9},{2,18},{26,10},{3,19},{27,11},{4,20},{... | collective-permute-start | bytes 1572872 | tf_op jit(solution)/shard_map/ppermute | solution.py:398
  264.0 36.6 %collective-permute-start.46 = (f32[1024,128]{1,0:T(8,128)S(1)}, f32[1024,128]{1,0:T(8,128)}, u32[]{:S(2)}, u32[]{:S(2)}) collective-permute-start(f32[1024,128]{1,0:T(8,128)S(1)} %collective-permute-done.44.refs_3_.refs_8_.refs_6_), channel_id=1, source_target_pairs={{0,16},{24,8},{1,17},{25,9},{2,18},{26,10},{3,19},{27,11},{4,20},{... | collective-permute-start | bytes 1572872 | tf_op jit(solution)/shard_map/ppermute | solution.py:398
  266.6 36.6 %collective-permute-start.51 = (f32[1024,128]{1,0:T(8,128)S(1)}, f32[1024,128]{1,0:T(8,128)}, u32[]{:S(2)}, u32[]{:S(2)}) collective-permute-start(f32[1024,128]{1,0:T(8,128)S(1)} %pad_maximum_fusion.25), channel_id=1, source_target_pairs={{0,8},{8,0},{16,24},{24,16},{1,9},{9,1},{17,25},{25,17},{2,10},{10... | collective-permute-start | bytes 1572872 | tf_op jit(solution)/shard_map/ppermute | solution.py:396
  273.5 31.9 %collective-permute-start.45 = (f32[1024,128]{1,0:T(8,128)S(1)}, f32[1024,128]{1,0:T(8,128)S(1)}, u32[]{:S(2)}, u32[]{:S(2)}) collective-permute-start(f32[1024,128]{1,0:T(8,128)S(1)} %collective-permute-done.44.refs_3_.refs_8_.refs_6_), channel_id=1, source_target_pairs={{0,1},{1,2},{2,3},{3,4},{4,5},{5,6},{6,7},{7,0},{8,9},{9,10},{10,1... | collective-permute-start | bytes 1572872 | tf_op jit(solution)/shard_map/ppermute | solution.py:407
  298.9 26.6 %collective-permute-start.42 = (f32[1024,128]{1,0:T(8,128)}, f32[1024,128]{1,0:T(8,128)S(1)}, u32[]{:S(2)}, u32[]{:S(2)}) collective-permute-start(f32[1024,128]{1,0:T(8,128)} %pad_maximum_fusion.21), channel_id=1, source_target_pairs={{0,8},{8,0},{16,24},{24,16},{1,9},{9,1},{17,25},{25,17},{2,10},{10... | collective-permute-start | bytes 1572872 | tf_op jit(solution)/shard_map/ppermute | solution.py:396
  300.6 27.0 %collective-permute-start.50 = (f32[1024,128]{1,0:T(8,128)}, f32[1024,128]{1,0:T(8,128)S(1)}, u32[]{:S(2)}, u32[]{:S(2)}) collective-permute-start(f32[1024,128]{1,0:T(8,128)} %collective-permute-done.41.refs_6_.refs_2_), channel_id=1, source_target_pairs={{0,16},{24,8},{1,17},{25,9},{2,18},{26,10},{3,19},{27,11},{4,20},{... | collective-permute-start | bytes 1572872 | tf_op jit(solution)/shard_map/ppermute | solution.py:398
  303.2 26.2 %collective-permute-start.52 = (f32[1024,128]{1,0:T(8,128)}, f32[1024,128]{1,0:T(8,128)S(1)}, u32[]{:S(2)}, u32[]{:S(2)}) collective-permute-start(f32[1024,128]{1,0:T(8,128)} %collective-permute-done.51.refs_8_.refs_4_), channel_id=1, source_target_pairs={{0,16},{24,8},{1,17},{25,9},{2,18},{26,10},{3,19},{27,11},{4,20},{... | collective-permute-start | bytes 1572872 | tf_op jit(solution)/shard_map/ppermute | solution.py:398
  305.5 23.9 %collective-permute-start.55 = (f32[1024,128]{1,0:T(8,128)}, f32[1024,128]{1,0:T(8,128)S(1)}, u32[]{:S(2)}, u32[]{:S(2)}) collective-permute-start(f32[1024,128]{1,0:T(8,128)} %pad_maximum_fusion.26), channel_id=1, source_target_pairs={{0,8},{8,0},{16,24},{24,16},{1,9},{9,1},{17,25},{25,17},{2,10},{10... | collective-permute-start | bytes 1572872 | tf_op jit(solution)/shard_map/ppermute | solution.py:396
  329.4 23.5 %collective-permute-start.56 = (f32[1024,128]{1,0:T(8,128)S(1)}, f32[1024,128]{1,0:T(8,128)S(1)}, u32[]{:S(2)}, u32[]{:S(2)}) collective-permute-start(f32[1024,128]{1,0:T(8,128)S(1)} %collective-permute-done.55.refs_8_.refs_4_), channel_id=1, source_target_pairs={{0,16},{24,8},{1,17},{25,9},{2,18},{26,10},{3,19},{27,11},{4,20},{... | collective-permute-start | bytes 1572872 | tf_op jit(solution)/shard_map/ppermute | solution.py:398
  330.7 22.1 %collective-permute-start.59 = (f32[1024,128]{1,0:T(8,128)S(1)}, f32[1024,128]{1,0:T(8,128)S(1)}, u32[]{:S(2)}, u32[]{:S(2)}) collective-permute-start(f32[1024,128]{1,0:T(8,128)S(1)} %pad_maximum_fusion.27), channel_id=1, source_target_pairs={{0,8},{8,0},{16,24},{24,16},{1,9},{9,1},{17,25},{25,17},{2,10},{10... | collective-permute-start | bytes 1572872 | tf_op jit(solution)/shard_map/ppermute | solution.py:396
  341.6 26.9 %collective-permute-start.53 = (f32[1024,128]{1,0:T(8,128)S(1)}, f32[1024,128]{1,0:T(8,128)S(1)}, u32[]{:S(2)}, u32[]{:S(2)}) collective-permute-start(f32[1024,128]{1,0:T(8,128)S(1)} %pad_maximum_fusion.19), channel_id=1, source_target_pairs={{0,8},{8,0},{16,24},{24,16},{1,9},{9,1},{17,25},{25,17},{2,10},{10... | collective-permute-start | bytes 1572872 | tf_op jit(solution)/shard_map/ppermute | solution.py:396
  343.6 27.0 %collective-permute-start.58 = (f32[1024,128]{1,0:T(8,128)S(1)}, f32[1024,128]{1,0:T(8,128)S(1)}, u32[]{:S(2)}, u32[]{:S(2)}) collective-permute-start(f32[1024,128]{1,0:T(8,128)S(1)} %collective-permute-done.49.refs_6_.refs_2_), channel_id=1, source_target_pairs={{0,16},{24,8},{1,17},{25,9},{2,18},{26,10},{3,19},{27,11},{4,20},{... | collective-permute-start | bytes 1572872 | tf_op jit(solution)/shard_map/ppermute | solution.py:398
  352.8 22.5 %collective-permute-start.60 = (f32[1024,128]{1,0:T(8,128)S(1)}, f32[1024,128]{1,0:T(8,128)S(1)}, u32[]{:S(2)}, u32[]{:S(2)}) collective-permute-start(f32[1024,128]{1,0:T(8,128)S(1)} %collective-permute-done.59.refs_8_.refs_4_), channel_id=1, source_target_pairs={{0,16},{24,8},{1,17},{25,9},{2,18},{26,10},{3,19},{27,11},{4,20},{... | collective-permute-start | bytes 1572872 | tf_op jit(solution)/shard_map/ppermute | solution.py:398
  357.7 17.7 %collective-permute-start.63 = (f32[1024,128]{1,0:T(8,128)S(1)}, f32[1024,128]{1,0:T(8,128)S(1)}, u32[]{:S(2)}, u32[]{:S(2)}) collective-permute-start(f32[1024,128]{1,0:T(8,128)S(1)} %pad_maximum_fusion.28), channel_id=1, source_target_pairs={{0,8},{8,0},{16,24},{24,16},{1,9},{9,1},{17,25},{25,17},{2,10},{10... | collective-permute-start | bytes 1572872 | tf_op jit(solution)/shard_map/ppermute | solution.py:396
  368.5 23.1 %collective-permute-start.57 = (f32[1024,128]{1,0:T(8,128)S(1)}, f32[1024,128]{1,0:T(8,128)S(1)}, u32[]{:S(2)}, u32[]{:S(2)}) collective-permute-start(f32[1024,128]{1,0:T(8,128)S(1)} %pad_maximum_fusion.18), channel_id=1, source_target_pairs={{0,8},{8,0},{16,24},{24,16},{1,9},{9,1},{17,25},{25,17},{2,10},{10... | collective-permute-start | bytes 1572872 | tf_op jit(solution)/shard_map/ppermute | solution.py:396
  370.6 23.1 %collective-permute-start.62 = (f32[1024,128]{1,0:T(8,128)S(1)}, f32[1024,128]{1,0:T(8,128)S(1)}, u32[]{:S(2)}, u32[]{:S(2)}) collective-permute-start(f32[1024,128]{1,0:T(8,128)S(1)} %collective-permute-done.53.refs_6_.refs_2_), channel_id=1, source_target_pairs={{0,16},{24,8},{1,17},{25,9},{2,18},{26,10},{3,19},{27,11},{4,20},{... | collective-permute-start | bytes 1572872 | tf_op jit(solution)/shard_map/ppermute | solution.py:398
  375.3 22.5 %collective-permute-start.64 = (f32[1024,128]{1,0:T(8,128)S(1)}, f32[1024,128]{1,0:T(8,128)S(1)}, u32[]{:S(2)}, u32[]{:S(2)}) collective-permute-start(f32[1024,128]{1,0:T(8,128)S(1)} %collective-permute-done.63.refs_8_.refs_4_), channel_id=1, source_target_pairs={{0,16},{24,8},{1,17},{25,9},{2,18},{26,10},{3,19},{27,11},{4,20},{... | collective-permute-start | bytes 1572872 | tf_op jit(solution)/shard_map/ppermute | solution.py:398
  379.7 18.1 %collective-permute-start.69 = (f32[1024,128]{1,0:T(8,128)S(1)}, f32[1024,128]{1,0:T(8,128)S(1)}, u32[]{:S(2)}, u32[]{:S(2)}) collective-permute-start(f32[1024,128]{1,0:T(8,128)S(1)} %pad_maximum_fusion.29), channel_id=1, source_target_pairs={{0,8},{8,0},{16,24},{24,16},{1,9},{9,1},{17,25},{25,17},{2,10},{10... | collective-permute-start | bytes 1572872 | tf_op jit(solution)/shard_map/ppermute | solution.py:396
  391.7 22.4 %collective-permute-start.61 = (f32[1024,128]{1,0:T(8,128)S(1)}, f32[1024,128]{1,0:T(8,128)S(1)}, u32[]{:S(2)}, u32[]{:S(2)}) collective-permute-start(f32[1024,128]{1,0:T(8,128)S(1)} %pad_maximum_fusion.17), channel_id=1, source_target_pairs={{0,8},{8,0},{16,24},{24,16},{1,9},{9,1},{17,25},{25,17},{2,10},{10... | collective-permute-start | bytes 1572872 | tf_op jit(solution)/shard_map/ppermute | solution.py:396
  393.7 22.4 %collective-permute-start.66 = (f32[1024,128]{1,0:T(8,128)S(1)}, f32[1024,128]{1,0:T(8,128)S(1)}, u32[]{:S(2)}, u32[]{:S(2)}) collective-permute-start(f32[1024,128]{1,0:T(8,128)S(1)} %collective-permute-done.57.refs_6_.refs_2_), channel_id=1, source_target_pairs={{0,16},{24,8},{1,17},{25,9},{2,18},{26,10},{3,19},{27,11},{4,20},{... | collective-permute-start | bytes 1572872 | tf_op jit(solution)/shard_map/ppermute | solution.py:398
  397.8 22.5 %collective-permute-start.70 = (f32[1024,128]{1,0:T(8,128)S(1)}, f32[1024,128]{1,0:T(8,128)S(1)}, u32[]{:S(2)}, u32[]{:S(2)}) collective-permute-start(f32[1024,128]{1,0:T(8,128)S(1)} %collective-permute-done.69.refs_8_.refs_4_), channel_id=1, source_target_pairs={{0,16},{24,8},{1,17},{25,9},{2,18},{26,10},{3,19},{27,11},{4,20},{... | collective-permute-start | bytes 1572872 | tf_op jit(solution)/shard_map/ppermute | solution.py:398
  402.2 18.1 %collective-permute-start.72 = (f32[1024,128]{1,0:T(8,128)S(1)}, f32[1024,128]{1,0:T(8,128)S(1)}, u32[]{:S(2)}, u32[]{:S(2)}) collective-permute-start(f32[1024,128]{1,0:T(8,128)S(1)} %pad_maximum_fusion.30), channel_id=1, source_target_pairs={{0,8},{8,0},{16,24},{24,16},{1,9},{9,1},{17,25},{25,17},{2,10},{10... | collective-permute-start | bytes 1572872 | tf_op jit(solution)/shard_map/ppermute | solution.py:396
  418.4 41.9 %collective-permute-start.79 = (f32[512,512]{1,0:T(8,128)S(1)}, f32[512,512]{1,0:T(8,128)S(1)}, u32[]{:S(2)}, u32[]{:S(2)}) collective-permute-start(f32[512,512]{1,0:T(8,128)S(1)} %copy-done.47), channel_id=1, source_target_pairs={{1,0},{2,1},{3,2},{4,3},{5,4},{6,5},{7,6},{0,7},{9,8},{10,9},{11,1... | collective-permute-start | bytes 3145736 | tf_op jit(solution)/shard_map/ppermute | solution.py:418
  420.2 27.6 %collective-permute-start.74 = (f32[1024,128]{1,0:T(8,128)S(1)}, f32[1024,128]{1,0:T(8,128)S(1)}, u32[]{:S(2)}, u32[]{:S(2)}) collective-permute-start(f32[1024,128]{1,0:T(8,128)S(1)} %collective-permute-done.72.refs_4_.refs_2_.refs_8_), channel_id=1, source_target_pairs={{0,16},{24,8},{1,17},{25,9},{2,18},{26,10},{3,19},{27,11},{4,20},{... | collective-permute-start | bytes 1572872 | tf_op jit(solution)/shard_map/ppermute | solution.py:398
  431.5 27.6 %collective-permute-start.68 = (f32[1024,128]{1,0:T(8,128)S(1)}, f32[1024,128]{1,0:T(8,128)S(1)}, u32[]{:S(2)}, u32[]{:S(2)}) collective-permute-start(f32[1024,128]{1,0:T(8,128)S(1)} %collective-permute-done.65.refs_6_.refs_4_.refs_2_), channel_id=1, source_target_pairs={{0,16},{24,8},{1,17},{25,9},{2,18},{26,10},{3,19},{27,11},{4,20},{... | collective-permute-start | bytes 1572872 | tf_op jit(solution)/shard_map/ppermute | solution.py:398
  435.9 24.5 %collective-permute-start.77 = (f32[1024,128]{1,0:T(8,128)S(1)}, f32[1024,128]{1,0:T(8,128)S(1)}, u32[]{:S(2)}, u32[]{:S(2)}) collective-permute-start(f32[1024,128]{1,0:T(8,128)S(1)} %copy-done.27), channel_id=1, source_target_pairs={{1,0},{2,1},{3,2},{4,3},{5,4},{6,5},{7,6},{0,7},{9,8},{10,9},{11,1... | collective-permute-start | bytes 1572872 | tf_op jit(solution)/shard_map/ppermute | solution.py:407
  436.0 24.4 %collective-permute-start.78 = (f32[1024,128]{1,0:T(8,128)S(1)}, f32[1024,128]{1,0:T(8,128)S(1)}, u32[]{:S(2)}, u32[]{:S(2)}) collective-permute-start(f32[1024,128]{1,0:T(8,128)S(1)} %copy-done.32), channel_id=1, source_target_pairs={{1,0},{2,1},{3,2},{4,3},{5,4},{6,5},{7,6},{0,7},{9,8},{10,9},{11,1... | collective-permute-start | bytes 1572872 | tf_op jit(solution)/shard_map/ppermute | solution.py:407
  456.6 26.7 %collective-permute-start.75 = (f32[512,128]{1,0:T(8,128)S(1)}, f32[512,128]{1,0:T(8,128)S(1)}, u32[]{:S(2)}, u32[]{:S(2)}) collective-permute-start(f32[512,128]{1,0:T(8,128)S(1)} %collective-permute-done.73.refs_8_), channel_id=1, source_target_pairs={{0,16},{24,8},{1,17},{25,9},{2,18},{26,10},{3,19},{27,11},{4,20},{... | collective-permute-start | bytes 786440 | tf_op jit(solution)/shard_map/ppermute | solution.py:398
  459.1 35.5 %collective-permute-start.76 = (f32[512,128]{1,0:T(8,128)S(1)}, f32[512,128]{1,0:T(8,128)S(1)}, u32[]{:S(2)}, u32[]{:S(2)}) collective-permute-start(f32[512,128]{1,0:T(8,128)S(1)} %collective-permute-done.71.refs_6_.refs_4_), channel_id=1, source_target_pairs={{0,16},{24,8},{1,17},{25,9},{2,18},{26,10},{3,19},{27,11},{4,20},{... | collective-permute-start | bytes 786440 | tf_op jit(solution)/shard_map/ppermute | solution.py:398
  (157 other events, 2300.1 us)

commit v2 on v1

--- a/solution.py
+++ b/solution.py
@@ -18,8 +18,10 @@
 OFFSETS = (0, 1, -1, 2, -2, REACH, -REACH)
 MIRROR = (0, 2, 1, 4, 3, 6, 5)
 IN_FLIGHT = 2
+DEFER = 1
+RELAYS = 2
 HOLD = 5
-VMEM = 28 * 2**20
+VMEM = 24 * 2**20
 
 
 def block_rates(win, lane, count, row, coef, coef_row, band, index, put):
@@ -73,11 +75,13 @@
     n_in, n_out = len(names), len(a_own) + (1 if b else 0)
     ref = dict(zip(names, refs[:n_in]))
     outs = refs[n_in : n_in + n_out]
-    win, mid, coef, band, feed, sems, out_sems, feed_sems = refs[n_in + n_out :]
+    coef = ref["coef"]
+    win, mid, band, feed, sems, out_sems, feed_sems = refs[n_in + n_out :]
     base = ref["base"][0]
     row_axis = lax.axis_index("row")
     odd = lax.rem(row_axis, 2)
     block_of = {"PF": 5 - 5 * odd, "PN": 4 - 3 * odd, "QN": 1 + 3 * odd, "QF": 5 * odd}
+    half_of = {"PF": 1 - odd, "PN": odd, "QN": 1 - odd, "QF": odd}
     row_first = row_axis * (2 * REACH)
     col_first = lax.axis_index("col") * cols
     own_rows = pl.ds(2 * REACH, 2 * REACH)
@@ -93,10 +97,11 @@
     def pair(first):
         return pl.ds(first * HALVES, HALVES)
 
-    def load_piece(kind, name, offset, tile, group):
+    def load_piece(kind, name, full, tile, group):
         start = pl.multiple_of(block_of[kind] * REACH, REACH)
+        at = pl.multiple_of(half_of[kind] * REACH, REACH) if full else 0
         for c in range(HALVES):
-            src = ref[name].at[pl.ds((offset + c) * REACH, REACH), :]
+            src = ref[name].at[pl.ds(at, REACH), pl.ds(c * LANES, LANES)]
             group.append(load(src, win.at[(tile - e_first) * HALVES + c, pl.ds(start, REACH), :]))
 
     band_tiles = sorted(set(a_own) | set(a_near) | set(b))
@@ -111,15 +116,10 @@
     for index, tile in enumerate(band_tiles):
         src = ref["band"].at[pl.ds((base + tile + 1) * HALVES, HALVES)]
         first.append(load(src, band.at[pair(index)]))
-    if a_own or b:
-        first.append(load(ref["coef"].at[:, mid_rows, :], coef.at[:, mid_rows, :]))
-    for kind, name, offset, tile in near_loads:
-        load_piece(kind, name, offset, tile, first if tile in a_own else second)
-    for kind, name, offset, tile in far_loads:
-        load_piece(kind, name, offset, tile, second)
-    if a_near:
-        for rows in (pl.ds(0, REACH), pl.ds(3 * REACH, REACH)):
-            second.append(load(ref["coef"].at[:, rows, :], coef.at[:, rows, :]))
+    for kind, name, full, tile in near_loads:
+        load_piece(kind, name, full, tile, first if tile in a_own else second)
+    for kind, name, full, tile in far_loads:
+        load_piece(kind, name, full, tile, second)
     for name, tile in mid_loads:
         third.append(load(ref[name], mid.at[pair(tile - m_first), mid_rows, :]))
 
@@ -232,6 +232,11 @@
     plan = key[:8] + (e_first, m_first, modes, slab_shape[1], fed)
     f32 = jnp.float32
     whole = pl.BlockSpec(memory_space=pl.ANY)
+    places = {"base": pl.BlockSpec(memory_space=pltpu.SMEM), "coef": pl.BlockSpec(memory_space=pltpu.VMEM)}
+    operands = [
+        v if n == "base" else pltpu.with_memory_space_constraint(v, pltpu.VMEM if n == "coef" else pltpu.HBM)
+        for n, v in zip(names, operands)
+    ]
     shapes = [jax.ShapeDtypeStruct((HALVES, 2 * REACH, LANES), f32) for _ in a_own]
     if b:
         shapes.append(jax.ShapeDtypeStruct(slab_shape, f32))
@@ -242,12 +247,11 @@
     return pl.pallas_call(
         functools.partial(tile_kernel, plan),
         out_shape=shapes,
-        in_specs=[pl.BlockSpec(memory_space=pltpu.SMEM) if n == "base" else whole for n in names],
+        in_specs=[places.get(n, whole) for n in names],
         out_specs=[whole] * len(shapes),
         scratch_shapes=[
             pltpu.VMEM((e_count * HALVES, 6 * REACH, LANES), f32),
             pltpu.VMEM((m_count * HALVES, 4 * REACH, LANES), f32),
-            pltpu.VMEM((7, 4 * REACH, LANES), f32),
             pltpu.VMEM((n_band * HALVES, 7, STRIP, LANES), f32),
             pltpu.VMEM((n_feeds, HALVES, REACH, LANES), f32),
             pltpu.SemaphoreType.DMA((n_loads,)),
@@ -264,16 +268,16 @@
 
 
 class Field:
-    def __init__(self, slab, coef, band, feed, modes):
-        self.slab, self.coef, self.band, self.feed, self.modes = slab, coef, band, feed, modes
+    def __init__(self, slab, modes):
+        self.slab, self.modes, self.feed = slab, modes, None
         self.tiles = slab.shape[1] // REACH
         self.parts = {}
         self.mids = {}
         self.out = None
         self.last = None
 
-    def step(self, base, a_own, a_near, b):
-        operands = {"base": jnp.full((1,), base, jnp.int32)}
+    def step(self, base, a_own, a_near, b, since):
+        operands = {"base": lax.optimization_barrier((jnp.full((1,), base, jnp.int32), since))[0]}
         own_loads, near_loads, far_loads, mid_loads = [], [], [], []
         for t in sorted({t + d for t in a_own for d in (-1, 0, 1)} | set(a_near) | set(b)):
             at = base + t
@@ -287,10 +291,11 @@
             own_loads.append((name, place, from_base, t))
 
         def piece(kind, t):
-            value, offset = self.parts[kind, base + t]
-            name = f"{kind if value.shape[0] == 2 * REACH else kind[0]}{t}"
+            value = self.parts[kind, base + t]
+            full = value.shape[0] == 2 * REACH
+            name = f"{kind[0] if full else kind}{t}"
             operands[name] = value
-            return kind, name, offset, t
+            return kind, name, full, t
 
         for t in sorted(set(a_own) | {t + d for t in a_near for d in (-1, 0, 1)}):
             near_loads += [piece(kind, t) for kind in ("PN", "QN")]
@@ -315,7 +320,7 @@
             self.mids[base + t] = value
         if b:
             self.out = results[-1]
-        self.last = results[0]
+        self.last = results[-1]
 
 
 def shards(g_start, cotangent, damping, hopping, bonds, source):
@@ -323,7 +328,7 @@
     modes = damping.shape[0]
     n_row, n_col = lax.axis_size("row"), lax.axis_size("col")
     tiles = cols_dev // REACH
-    assert rows_dev == 2 * REACH and cols_dev % REACH == 0 and tiles >= 3 and n_row % 2 == 0
+    assert rows_dev == 2 * REACH and cols_dev % (2 * REACH) == 0 and tiles >= 4 and n_row % 2 == 0
     row_axis = lax.axis_index("row")
     odd = lax.rem(row_axis, 2)
     row_first = row_axis * rows_dev
@@ -343,96 +348,169 @@
         turned = [coef[m, REACH + o : REACH + o + count] for m, o in zip(MIRROR, OFFSETS)]
         return coef[:, REACH : REACH + count], jnp.stack(turned)
 
-    count = 4 * REACH
-    inside = row_first - REACH + lax.iota(jnp.int32, count)
-    inside = (inside >= 0) & (inside < n_row * rows_dev)
-    feed = jnp.where(inside[None, :], ring(source, row_first - REACH, count), 0.0)
-    shape = (4, 3, HALVES, REACH, LANES)
-    axis = functools.partial(lax.broadcasted_iota, jnp.int32, shape)
-    rel = (axis(1) - 1) * REACH + axis(2) * LANES + axis(4) - axis(3)
-    dense = jnp.zeros(shape, jnp.float32)
-    for k, offset in enumerate(OFFSETS):
-        dense = dense + jnp.where(rel == offset, feed[k].reshape(4, 1, 1, REACH, 1), 0.0)
-    row_coefs = gathered(row_first - REACH, count)
-    col_coefs = gathered(col_first - REACH, cols_dev + 2 * REACH)
-
-    def row_table(coef):
-        coef = jnp.where(inside[None, :], coef, 0.0)
-        return jnp.broadcast_to(coef[:, :, None], (7, count, LANES))
-
-    def col_table(coef):
-        coef = coef.reshape(7, (tiles + 2) * HALVES, 1, LANES).transpose(1, 0, 2, 3)
-        return jnp.broadcast_to(coef, ((tiles + 2) * HALVES, 7, STRIP, LANES))
-
-    fields = [
-        Field(slab, row_table(row), col_table(col), fed, modes)
-        for slab, row, col, fed in zip((g_start, cotangent), row_coefs, col_coefs, (dense, None))
-    ]
-
     swap = [(i, i ^ 1) for i in range(n_row)]
     relay = [(i, i + 2) for i in range(0, n_row - 2, 2)] + [(i, i - 2) for i in range(3, n_row, 2)]
     to_right = [(i, (i + 1) % n_col) for i in range(n_col)]
     to_left = [((i + 1) % n_col, i) for i in range(n_col)]
 
+    fields = [Field(slab, modes) for slab in (g_start, cotangent)]
     swapped, relayed = [], []
-    holds = {}
-
-    def after(value, others):
+    holds, relay_holds = {}, {}
+
+    def after(value, *others):
         others = [other for other in others if other is not None]
         if not others:
             return value
         return lax.optimization_barrier((value, *others))[0]
 
-    def exchange(field, tile, halves):
-        pieces = []
-        for half in halves:
+    def past(chain, index, lag):
+        return chain[index - lag] if index >= lag else None
+
+    def exchange(field, tile, half=None):
+        index = len(swapped)
+        slab = field.slab if field is fields[0] else after(field.slab, swapped[0])
+        if half is None:
+            piece = slab[:, tile * REACH : (tile + 1) * REACH]
+        else:
             start = (odd if half == 0 else 1 - odd) * REACH
-            for c in range(HALVES):
-                at = (start, tile * REACH + c * LANES)
-                pieces.append(lax.dynamic_slice(field.slab, at, (REACH, LANES)))
-        piece = jnp.concatenate(pieces, axis=0)
-        index = len(swapped)
-        earlier = swapped[index - IN_FLIGHT] if index >= IN_FLIGHT else None
-        got = lax.ppermute(after(piece, [earlier, holds.pop(index, None)]), "row", swap)
-        earlier = relayed[index - IN_FLIGHT] if index >= IN_FLIGHT else None
-        passed = lax.ppermute(after(got, [earlier]), "row", relay)
+            piece = lax.dynamic_slice(slab, (start, tile * REACH), (REACH, REACH))
+        got = lax.ppermute(after(piece, past(swapped, index, IN_FLIGHT), *holds.pop(index, ())), "row", swap)
+        passed = lax.ppermute(after(got, past(relayed, index, RELAYS), *relay_holds.pop(index, ())), "row", relay)
         swapped.append(got)
         relayed.append(passed)
-        for place, half in enumerate(halves):
-            field.parts["PN" if half else "PF", tile] = got, place * HALVES
-            field.parts["QF" if half else "QN", tile] = passed, place * HALVES
-
-    def edge(field, source_tile, target_tile, route):
-        for kinds in (("PF", "PN"), ("QN", "QF")):
-            moved = lax.ppermute(field.parts[kinds[0], source_tile][0], "col", route)
-            for place, kind in enumerate(kinds):
-                field.parts[kind, target_tile] = moved, place * HALVES
-
-    for field in fields:
-
-        def step(*args, field=field):
-            field.step(*args)
-            holds[len(swapped) - 1 + HOLD] = field.last
-
-        field.left = lax.ppermute(field.slab[:, cols_dev - 2 * REACH :], "col", to_right)
-        field.right = lax.ppermute(field.slab[:, : 2 * REACH], "col", to_left)
-        last = tiles - 2
-        exchange(field, 0, (0, 1))
-        edge(field, 0, tiles, to_left)
-        exchange(field, tiles - 1, (0, 1))
-        edge(field, tiles - 1, -1, to_right)
-        step(0, (-1, 0), (), ())
-        for tile in range(1, last):
-            exchange(field, tile, (0, 1))
-            if tile % 2 == 0:
-                step(tile, (-1, 0), (-2, -1), (-2, -1))
-            elif tile == last - 1:
-                step(tile, (0,), (-1,), (-1,))
-        exchange(field, last, (0,))
-        exchange(field, last, (1,))
-        step(last, (1, 2), (), ())
-        step(last, (0,), (-1, 1), (-1, 1))
-        step(last, (), (0,), (0,))
+        for kind, of_half, value in (("PF", 0, got), ("PN", 1, got), ("QN", 0, passed), ("QF", 1, passed)):
+            if half in (None, of_half):
+                field.parts[kind, tile] = value
+
+    def step(field, *args, lag=HOLD):
+        field.step(*args, swapped[-1])
+        index = len(swapped) - 1
+        if index + lag < len(pieces):
+            holds.setdefault(index + lag, []).append(field.last)
+        elif index + 2 < len(pieces):
+            relay_holds.setdefault(index + 2, []).append(field.last)
+
+    raw = (damping, hopping, bonds, source)
+
+    def prepare():
+        damping, hopping, bonds, source = lax.optimization_barrier((*raw, swapped[0]))[:4]
+        count = 4 * REACH
+        inside = row_first - REACH + lax.iota(jnp.int32, count)
+        inside = (inside >= 0) & (inside < n_row * rows_dev)
+        feed = jnp.where(inside[None, :], ring(source, row_first - REACH, count), 0.0)
+        shape = (4, 3, HALVES, REACH, LANES)
+        axis = functools.partial(lax.broadcasted_iota, jnp.int32, shape)
+        rel = (axis(1) - 1) * REACH + axis(2) * LANES + axis(4) - axis(3)
+        dense = jnp.zeros(shape, jnp.float32)
+        for k, offset in enumerate(OFFSETS):
+            dense = dense + jnp.where(rel == offset, feed[k].reshape(4, 1, 1, REACH, 1), 0.0)
+        row_coefs = gathered(row_first - REACH, count)
+        col_coefs = gathered(col_first - REACH, cols_dev + 2 * REACH)
+
+        def row_table(coef):
+            coef = jnp.where(inside[None, :], coef, 0.0)
+            return jnp.broadcast_to(coef[:, :, None], (7, count, LANES))
+
+        def col_table(coef):
+            coef = coef.reshape(7, (tiles + 2) * HALVES, 1, LANES).transpose(1, 0, 2, 3)
+            return jnp.broadcast_to(coef, ((tiles + 2) * HALVES, 7, STRIP, LANES))
+
+        for field, row, col in zip(fields, row_coefs, col_coefs):
+            field.coef, field.band = row_table(row), col_table(col)
+        fields[0].feed = dense
+
+
+    forward, adjoint = fields
+    last = tiles - 2
+
+    def side(field, right):
+        route, name = (to_right, "left") if right else (to_left, "right")
+        first = cols_dev - 2 * REACH if right else 0
+
+        def send():
+            slab = after(field.slab, swapped[0])
+            setattr(field, name, lax.ppermute(after(slab[:, first : first + 2 * REACH], swapped[-1]), "col", route))
+
+        return send
+
+    def edge(field, kind, right):
+        source_tile, target_tile, route = (tiles - 1, -1, to_right) if right else (0, tiles, to_left)
+
+        def send():
+            value = after(field.parts[kind, source_tile], swapped[-1])
+            field.parts[kind, target_tile] = lax.ppermute(value, "col", route)
+
+        return send
+
+    def call(*args, **kwargs):
+        return lambda: step(*args, **kwargs)
+
+    pieces = []
+    extra = [(forward, 0), (forward, tiles - 1), (adjoint, 0), (adjoint, tiles - 1)]
+    for tile in range(1, last + 1):
+        work = []
+        if tile == 2:
+            work = [call(forward, 2, (-1, 0), (), ())]
+        elif tile % 2 == 0:
+            work = [call(forward, tile, (-1, 0), (-2, -1), (-2, -1))]
+        pieces.append((forward, tile, None, work))
+        if tile % 2 == 0 and extra:
+            pieces.append((*extra.pop(0), None, []))
+    pieces += [(*one, None, []) for one in extra]
+    for tile in range(1, last):
+        work = []
+        if tile == last - 1:
+            work = [call(adjoint, tile, (0,), (-1,), (-1,))]
+        elif tile % 2 == 0:
+            work = [call(adjoint, tile, (-1, 0), (-2, -1), (-2, -1))]
+        pieces.append((adjoint, tile, None, work))
+    pieces.append((adjoint, last, 0, []))
+    pieces.append(
+        (adjoint, last, 1, [call(adjoint, last, (0,), (-1, 1), (-1, 1)), call(adjoint, last, (), (0,), (0,))])
+    )
+    sides = [side(forward, True), side(forward, False)]
+    sides += [edge(forward, kind, right) for right in (False, True) for kind in ("PN", "QN")]
+    sides += [side(adjoint, True), side(adjoint, False)]
+    sides += [edge(adjoint, kind, right) for right in (False, True) for kind in ("PN", "QN")]
+    ends = [place for place, one in enumerate(pieces) if one[0] is forward and one[1] == last][0]
+    late = [
+        (4, 6, call(forward, 1, (-2, -1), (-1, 0), (-1, 0))),
+        (ends, 6, call(forward, last, (1, 2), (0, 1), (0, 1))),
+        (0, 12, call(adjoint, 0, (-1, 0), (), ())),
+        (0, 12, call(adjoint, tiles - 1, (0, 1), (), ())),
+    ]
+
+    def needs(index):
+        owner = {2: 0, 3: 0, 4: 1, 5: 1, 8: 2, 9: 2, 10: 3, 11: 3}.get(index)
+        if owner is None:
+            return 0
+        field, tile = [(forward, 0), (forward, tiles - 1), (adjoint, 0), (adjoint, tiles - 1)][owner]
+        return [place for place, one in enumerate(pieces) if one[:2] == (field, tile)][0] + 1
+
+    count_sent = 0
+    waiting = []
+    few = tiles < 8
+    for place, (field, tile, half, work) in enumerate(pieces):
+        exchange(field, tile, half)
+        if place == 0:
+            prepare()
+        while count_sent < len(sides) and place >= needs(count_sent):
+            sides[count_sent]()
+            count_sent += 1
+            if place < len(pieces) - 4 and not few:
+                break
+        final = place == len(pieces) - 1
+        waiting += [(place + DEFER, one) for one in work]
+        outer = [one for one in late if place > one[0] + DEFER and count_sent >= one[1]]
+        due = [one for one in waiting if final or one[0] <= place]
+        if not final and not few:
+            outer = [] if due else outer[:1]
+        for one in outer:
+            one[2]()
+            late.remove(one)
+        for one in due:
+            one[1]()
+            waiting.remove(one)
     return tuple(field.out for field in fields)
 
 

time: 511 us -> 472 us (0.924)
  Pallas kernels: 200 us -> 158 us
  waiting for transfers between devices: 81.1 us -> 107 us
  other arithmetic: 27.1 us -> 7.29 us
    pallas_call x22 -> x20, Pallas kernels: 200 us -> 158 us  [run_tiles(): pl.pallas_call(functools.partial(tile_kernel, plan), out_shape=shapes, in...]
    ppermute x80 -> x78, waiting for transfers between devices: 81.1 us -> 107 us  [the longest x33 96.5 us: exchange(): lax.ppermute(after(piece, past(swapped, index, IN_FLIGHT), *holds.pop(ind...]
    concatenate x33 -> x0, other arithmetic: 14.7 us -> none  [exchange(): piece = jnp.concatenate(pieces, axis=0)]
    dynamic_slice x2 -> x1, local copies, waits for them, and re-layouts: 10.9 us -> 1.07 us  [exchange(): piece = lax.dynamic_slice(slab, (start, tile * REACH), (REACH, REACH))]
    slice x3 -> x5, local copies, waits for them, and re-layouts: 4.6 us -> 12.9 us  [the longest x2 9.82 us: exchange(): piece = slab[:, tile * REACH:(tile + 1) * REACH]]
    unnamed x282 -> x284, local copies, waits for them, and re-layouts: 25.3 us -> 29.2 us
    ppermute x80 -> x78, starting transfers between devices: 139 us -> 136 us  [the longest x33 97.6 us: exchange(): lax.ppermute(after(got, past(relayed, index, RELAYS), *relay_holds.pop(in...]
  transfers between devices with their start and end apart: 80 -> 78, of which waited for: 17 -> 24; matrix products, arithmetic and copies ran while one was open for 9% -> 5% of each run, Pallas kernels for 39% -> 33%
where the time goes in v2:
time: 472 us; the launch traced here: 463 us
  Pallas kernels  158 us (33%)
  starting transfers between devices  136 us (29%)
  waiting for transfers between devices  107 us (23%)
  local copies, waits for them, and re-layouts  50.2 us (11%)
  other arithmetic  7.29 us (2%)
    pallas_call x20, Pallas kernels, run_tiles(): pl.pallas_call(functools.partial(tile_kernel, plan), out_shape=shapes, in...  158 us
    ppermute x33, starting transfers between devices, exchange(): lax.ppermute(after(got, past(relayed, index, RELAYS), *relay_holds.pop(in...  97.6 us
    ppermute x33, waiting for transfers between devices, exchange(): lax.ppermute(after(piece, past(swapped, index, IN_FLIGHT), *holds.pop(ind...  96.5 us
    ppermute x33, starting transfers between devices, exchange(): lax.ppermute(after(piece, past(swapped, index, IN_FLIGHT), *holds.pop(ind...  31.4 us
    unnamed x284, local copies, waits for them, and re-layouts  29.2 us
    ppermute x33, waiting for transfers between devices, exchange(): lax.ppermute(after(got, past(relayed, index, RELAYS), *relay_holds.pop(in...  10.7 us
    slice x2, local copies, waits for them, and re-layouts, exchange(): piece = slab[:, tile * REACH:(tile + 1) * REACH]  9.82 us
  transfers between devices with their start and end apart: 78, of which 24 were waited for; matrix products, arithmetic and copies ran while one was open for 5% of the time, Pallas kernels for 33%

profile of v2, /device:TPU:0, one launch (start us, length us, event | category | flops | bytes accessed | tf_op | source)
XLA Modules:
  0.0 462.5 jit_solution(5689239939278758724)
XLA Ops:
  0.6 6.9 %fusion.15 = (f32[512,256]{1,0:T(8,128)}, f32[512,256]{1,0:T(8,128)}, f32[512,256]{1,0:T(8,128)}, f32[512,256]{1,0:T(8,128)}, f32[512,256]{1,0:T(8,128)}, /*inde...) fusion(f32[512,4096]{1,0:T(8,128)} %refs_1_.24), kind=kLoop, calls=%fused_computation.43 | loop fusion | bytes 16777216 | tf_op jit(solution)/shard_map/slice | solution.py:373
  7.5 3.0 collective-permute-start
  13.9 9.5 %collective-permute-done.refs_2_.refs_7_ = f32[512,256]{1,0:T(8,128)S(1)} collective-permute-done((f32[512,256]{1,0:T(8,128)}, f32[512,256]{1,0:T(8,128)S(1)}, u32[]{:S(2)}, u32[]{:S(2)}) %collective-permute-start) | collective-permute-done | bytes 524320 | tf_op jit(solution)/shard_map/ppermute | solution.py:377
  26.1 8.6 %collective-permute-done.1.refs_4_.refs_9_ = f32[512,256]{1,0:T(8,128)S(1)} collective-permute-done((f32[512,256]{1,0:T(8,128)}, f32[512,256]{1,0:T(8,128)S(1)}, u32[]{:S(2)}, u32[]{:S(2)}) %collective-permute-start.1) | collective-permute-done | bytes 524320 | tf_op jit(solution)/shard_map/ppermute | solution.py:377
  36.8 3.4 collective-permute-start.5
  42.3 3.6 collective-permute-done.4.refs_5_
  50.4 2.8 fusion.16
  53.2 4.0 collective-permute-done.2.refs_6_.refs_2_
  60.3 4.4 collective-permute-start.13
  66.1 2.3 collective-permute-done.10.refs_8_.refs_4_
  70.5 3.7 select_add_fusion.refs_8_.refs_14_.refs_15_
  76.3 6.1 %run_tiles.10 = (f32[2,512,128]{2,1,0:T(8,128)S(1)}, f32[2,512,128]{2,1,0:T(8,128)S(1)}) custom-call(s32[1]{0:T(128)} %constant.29.clone.1.refs_0_, f32[512,4096]{1,0:T(8,128)} %refs_1_.24, f32[512,256]{1,0:T(8,128)} %copy-done.39, f32[512,256]{1,0:T(8,128)} %copy-done.41, f32[512,256]{1,0:T(8,128)} %copy-done.40, f32[512,256]{1,0:T(8,128)} %copy-done.42, ...), custom_call_target="tpu_custom_call" | custom-call | flops 7340032 | bytes 10485760 | tf_op jit(solution)/shard_map/jit(run_tiles)/pallas_call | solution.py:247
  84.2 4.1 collective-permute-start.15
  89.7 2.9 fusion.13
  93.0 9.2 %collective-permute-done.7.refs_8_.refs_4_ = f32[512,256]{1,0:T(8,128)S(1)} collective-permute-done((f32[512,256]{1,0:T(8,128)S(1)}, f32[512,256]{1,0:T(8,128)S(1)}, u32[]{:S(2)}, u32[]{:S(2)}) %collective-permute-start.7) | collective-permute-done | bytes 524320 | tf_op jit(solution)/shard_map/ppermute | solution.py:377
  104.2 3.4 collective-permute-start.16
  107.7 2.6 collective-permute-done.17.refs_8_
  110.3 4.4 collective-permute-start.18
  116.5 9.1 %run_tiles.11 = (f32[2,512,128]{2,1,0:T(8,128)S(1)}, f32[2,512,128]{2,1,0:T(8,128)S(1)}, f32[512,4096]{1,0:T(8,128)}) custom-call(s32[1]{0:T(128)} %constant.73.clone.1.refs_0_, f32[512,4096]{1,0:T(8,128)} %refs_1_.24, f32[512,256]{1,0:T(8,128)} %copy-done.39, f32[512,256]{1,0:T(8,128)} %copy-done.41, f32[512,256]{1,0:T(8,128)} %copy-done.40, ...), custom_call_target="tpu_custom_call" | custom-call | flops 22020096 | bytes 31457280 | tf_op jit(solution)/shard_map/jit(run_tiles)/pallas_call | solution.py:247
  130.3 4.4 collective-permute-start.29
  136.9 9.2 %run_tiles.12 = (f32[2,512,128]{2,1,0:T(8,128)}, f32[2,512,128]{2,1,0:T(8,128)}, f32[512,4096]{1,0:T(8,128)}) custom-call(s32[1]{0:T(128)} %constant.74.clone.1.refs_0_, f32[512,512]{1,0:T(8,128)} %copy-done.100, f32[512,4096]{1,0:T(8,128)} %refs_1_.24, f32[512,256]{1,0:T(8,128)} %copy-done.113, ...), custom_call_target="tpu_custom_call", output_to_operand_aliasing={{2}: (16, {})} | custom-call | flops 22020096 | bytes 31457280 | tf_op jit(solution)/shard_map/jit(run_tiles)/pallas_call | solution.py:247
  146.2 9.1 %run_tiles.20 = (f32[2,512,128]{2,1,0:T(8,128)S(1)}, f32[2,512,128]{2,1,0:T(8,128)S(1)}, f32[512,4096]{1,0:T(8,128)}) custom-call(s32[1]{0:T(128)} %constant.72.clone.1.refs_0_, f32[512,4096]{1,0:T(8,128)} %refs_1_.24, f32[512,256]{1,0:T(8,128)} %copy-done.67, f32[512,256]{1,0:T(8,128)} %copy-done.69, ...), custom_call_target="tpu_custom_call", output_to_operand_aliasing={{2}: (15, {})} | custom-call | flops 22020096 | bytes 31457280 | tf_op jit(solution)/shard_map/jit(run_tiles)/pallas_call | solution.py:247
  156.1 2.1 collective-permute-start.22
  161.7 2.1 collective-permute-done.26.refs_6_.refs_2_
  164.0 11.0 %collective-permute-done.22.refs_8_.refs_4_ = f32[512,256]{1,0:T(8,128)S(1)} collective-permute-done((f32[512,256]{1,0:T(8,128)S(1)}, f32[512,256]{1,0:T(8,128)S(1)}, u32[]{:S(2)}, u32[]{:S(2)}) %collective-permute-start.22) | collective-permute-done | bytes 524320 | tf_op jit(solution)/shard_map/ppermute | solution.py:377
  176.0 2.7 collective-permute-done.32.refs_4_.refs_9_.refs_7_
  178.7 4.4 collective-permute-start.31
  183.1 3.1 collective-permute-done.27.refs_6_.refs_2_
  186.3 2.4 collective-permute-start.33
  188.7 7.8 %collective-permute-done.23.refs_8_.refs_4_ = f32[512,256]{1,0:T(8,128)S(1)} collective-permute-done((f32[512,256]{1,0:T(8,128)S(1)}, f32[512,256]{1,0:T(8,128)S(1)}, u32[]{:S(2)}, u32[]{:S(2)}) %collective-permute-start.23) | collective-permute-done | bytes 524320 | tf_op jit(solution)/shard_map/ppermute | solution.py:377
  198.2 9.0 %run_tiles.21 = (f32[2,512,128]{2,1,0:T(8,128)S(1)}, f32[2,512,128]{2,1,0:T(8,128)S(1)}, f32[512,4096]{1,0:T(8,128)}) custom-call(s32[1]{0:T(128)} %constant.76.clone.1.refs_0_, f32[512,4096]{1,0:T(8,128)} %refs_1_.24, f32[512,256]{1,0:T(8,128)} %copy-done.49, f32[512,256]{1,0:T(8,128)} %copy-done.58, ...), custom_call_target="tpu_custom_call", output_to_operand_aliasing={{2}: (15, {})} | custom-call | flops 22020096 | bytes 31457280 | tf_op jit(solution)/shard_map/jit(run_tiles)/pallas_call | solution.py:247
  212.9 2.9 collective-permute-start.37
  217.7 8.2 %collective-permute-done.24.refs_5_.refs_8_ = f32[512,256]{1,0:T(8,128)S(1)} collective-permute-done((f32[512,256]{1,0:T(8,128)}, f32[512,256]{1,0:T(8,128)S(1)}, u32[]{:S(2)}, u32[]{:S(2)}) %collective-permute-start.24) | collective-permute-done | bytes 524320 | tf_op jit(solution)/shard_map/ppermute | solution.py:377
  228.4 4.5 run_tiles.13
  232.9 9.3 %run_tiles.22 = (f32[2,512,128]{2,1,0:T(8,128)S(1)}, f32[2,512,128]{2,1,0:T(8,128)S(1)}, f32[512,4096]{1,0:T(8,128)}) custom-call(s32[1]{0:T(128)} %constant.75.clone.1.refs_0_, f32[512,4096]{1,0:T(8,128)} %refs_1_.24, f32[512,256]{1,0:T(8,128)} %copy-done.47, f32[512,256]{1,0:T(8,128)} %copy-done.57, ...), custom_call_target="tpu_custom_call", output_to_operand_aliasing={{2}: (15, {})} | custom-call | flops 22020096 | bytes 31457280 | tf_op jit(solution)/shard_map/jit(run_tiles)/pallas_call | solution.py:247
  246.1 2.9 collective-permute-start.38
  251.2 3.9 run_tiles.15
  256.8 9.1 %run_tiles.23 = (f32[2,512,128]{2,1,0:T(8,128)S(1)}, f32[2,512,128]{2,1,0:T(8,128)S(1)}, f32[512,4096]{1,0:T(8,128)}) custom-call(s32[1]{0:T(128)} %constant.78.clone.1.refs_0_, f32[512,4096]{1,0:T(8,128)} %refs_1_.24, f32[512,256]{1,0:T(8,128)} %copy-done.51, f32[512,256]{1,0:T(8,128)} %copy-done.61, ...), custom_call_target="tpu_custom_call", output_to_operand_aliasing={{2}: (15, {})} | custom-call | flops 22020096 | bytes 31457280 | tf_op jit(solution)/shard_map/jit(run_tiles)/pallas_call | solution.py:247
  270.3 4.5 collective-permute-start.57
  276.1 6.2 %collective-permute-done.63.refs_8_.refs_4_ = f32[512,256]{1,0:T(8,128)S(1)} collective-permute-done((f32[512,256]{1,0:T(8,128)S(1)}, f32[512,256]{1,0:T(8,128)S(1)}, u32[]{:S(2)}, u32[]{:S(2)}) %collective-permute-start.63) | collective-permute-done | bytes 524320 | tf_op jit(solution)/shard_map/ppermute | solution.py:377
  282.4 10.0 %collective-permute-done.50.refs_6_.refs_2_ = f32[512,256]{1,0:T(8,128)S(1)} collective-permute-done((f32[512,256]{1,0:T(8,128)S(1)}, f32[512,256]{1,0:T(8,128)S(1)}, u32[]{:S(2)}, u32[]{:S(2)}) %collective-permute-start.50) | collective-permute-done | bytes 524320 | tf_op jit(solution)/shard_map/ppermute | solution.py:377
  296.0 4.4 collective-permute-start.58
  300.4 9.2 %run_tiles.24 = (f32[2,512,128]{2,1,0:T(8,128)S(1)}, f32[2,512,128]{2,1,0:T(8,128)S(1)}, f32[512,4096]{1,0:T(8,128)}) custom-call(s32[1]{0:T(128)} %constant.28.clone.1.refs_0_, f32[512,4096]{1,0:T(8,128)} %refs_1_.24, f32[512,256]{1,0:T(8,128)} %copy-done.48, f32[512,256]{1,0:T(8,128)} %copy-done.60, ...), custom_call_target="tpu_custom_call", output_to_operand_aliasing={{2}: (15, {})} | custom-call | flops 22020096 | bytes 31457280 | tf_op jit(solution)/shard_map/jit(run_tiles)/pallas_call | solution.py:247
  311.4 3.4 collective-permute-start.67
  315.7 8.9 %run_tiles.14 = (f32[2,512,128]{2,1,0:T(8,128)}, f32[2,512,128]{2,1,0:T(8,128)}, f32[512,4096]{1,0:T(8,128)}) custom-call(s32[1]{0:T(128)} %constant.28.clone.1.refs_0_, f32[512,4096]{1,0:T(8,128)} %refs_1_.24, f32[512,512]{1,0:T(8,128)} %copy-done.102, f32[512,256]{1,0:T(8,128)} %copy-done.56, ...), custom_call_target="tpu_custom_call", output_to_operand_aliasing={{2}: (16, {})} | custom-call | flops 22020096 | bytes 31457280 | tf_op jit(solution)/shard_map/jit(run_tiles)/pallas_call | solution.py:247
  324.7 4.4 collective-permute-start.59
  329.2 8.9 %run_tiles.16 = (f32[2,512,128]{2,1,0:T(8,128)S(1)}, f32[2,512,128]{2,1,0:T(8,128)S(1)}, f32[512,4096]{1,0:T(8,128)}) custom-call(s32[1]{0:T(128)} %constant.29.clone.1.refs_0_, f32[512,4096]{1,0:T(8,128)} %refs_1_.29, f32[512,256]{1,0:T(8,128)} %copy-done.73, f32[512,256]{1,0:T(8,128)} %copy-done.74, f32[512,256]{1,0:T(8,128)} %collective-permute-done.12.refs_5_.refs_4_, ...), custom_call_target="tpu_custom_call" | custom-call | flops 22020096 | bytes 31457280 | tf_op jit(solution)/shard_map/jit(run_tiles)/pallas_call | solution.py:247
  339.8 3.4 collective-permute-start.68
  343.4 4.6 collective-permute-start.60
  348.1 8.9 %run_tiles.25 = (f32[2,512,128]{2,1,0:T(8,128)S(1)}, f32[2,512,128]{2,1,0:T(8,128)S(1)}, f32[512,4096]{1,0:T(8,128)}) custom-call(s32[1]{0:T(128)} %constant.73.clone.1.refs_0_, f32[512,4096]{1,0:T(8,128)} %refs_1_.29, f32[512,256]{1,0:T(8,128)} %copy-done.78, f32[512,256]{1,0:T(8,128)} %copy-done.89, ...), custom_call_target="tpu_custom_call", output_to_operand_aliasing={{2}: (14, {})} | custom-call | flops 22020096 | bytes 31457280 | tf_op jit(solution)/shard_map/jit(run_tiles)/pallas_call | solution.py:247
  358.7 3.4 collective-permute-start.69
  362.2 3.7 collective-permute-done.53.refs_6_.refs_2_
  366.9 4.4 collective-permute-start.61
  371.3 8.8 %run_tiles.26 = (f32[2,512,128]{2,1,0:T(8,128)S(1)}, f32[2,512,128]{2,1,0:T(8,128)S(1)}, f32[512,4096]{1,0:T(8,128)}) custom-call(s32[1]{0:T(128)} %constant.72.clone.1.refs_0_, f32[512,4096]{1,0:T(8,128)} %refs_1_.29, f32[512,256]{1,0:T(8,128)} %copy-done.80, f32[512,256]{1,0:T(8,128)} %copy-done.87, ...), custom_call_target="tpu_custom_call", output_to_operand_aliasing={{2}: (14, {})} | custom-call | flops 22020096 | bytes 31457280 | tf_op jit(solution)/shard_map/jit(run_tiles)/pallas_call | solution.py:247
  381.9 4.9 %collective-permute-start.71 = (f32[512,256]{1,0:T(8,128)S(1)}, f32[512,256]{1,0:T(8,128)}, u32[]{:S(2)}, u32[]{:S(2)}) collective-permute-start(f32[512,256]{1,0:T(8,128)S(1)} %collective-permute-done.70.refs_8_.refs_4_), channel_id=1, source_target_pairs={{0,16},{24,8},{1,17},{25,9},{2,18},{26,10},{3,19},{27,11},{4,20},{... | collective-permute-start | bytes 1572872 | tf_op jit(solution)/shard_map/ppermute | solution.py:378
  389.3 4.4 collective-permute-start.62
  396.9 8.8 %run_tiles.27 = (f32[2,512,128]{2,1,0:T(8,128)S(1)}, f32[2,512,128]{2,1,0:T(8,128)S(1)}, f32[512,4096]{1,0:T(8,128)}) custom-call(s32[1]{0:T(128)} %constant.76.clone.1.refs_0_, f32[512,4096]{1,0:T(8,128)} %refs_1_.29, f32[512,256]{1,0:T(8,128)} %copy-done.75, f32[512,256]{1,0:T(8,128)} %copy-done.86, ...), custom_call_target="tpu_custom_call", output_to_operand_aliasing={{2}: (14, {})} | custom-call | flops 22020096 | bytes 31457280 | tf_op jit(solution)/shard_map/jit(run_tiles)/pallas_call | solution.py:247
  408.9 8.8 %run_tiles.28 = (f32[2,512,128]{2,1,0:T(8,128)S(1)}, f32[2,512,128]{2,1,0:T(8,128)S(1)}, f32[512,4096]{1,0:T(8,128)}) custom-call(s32[1]{0:T(128)} %constant.75.clone.1.refs_0_, f32[512,4096]{1,0:T(8,128)} %refs_1_.29, f32[512,256]{1,0:T(8,128)} %copy-done.82, f32[512,256]{1,0:T(8,128)} %copy-done.90, ...), custom_call_target="tpu_custom_call", output_to_operand_aliasing={{2}: (14, {})} | custom-call | flops 22020096 | bytes 31457280 | tf_op jit(solution)/shard_map/jit(run_tiles)/pallas_call | solution.py:247
  422.8 4.3 collective-permute-done.74.refs_8_
  427.1 2.1 collective-permute-start.76
  429.3 9.0 %run_tiles.29 = (f32[2,512,128]{2,1,0:T(8,128)S(1)}, f32[2,512,128]{2,1,0:T(8,128)S(1)}, f32[512,4096]{1,0:T(8,128)}) custom-call(s32[1]{0:T(128)} %constant.78.clone.1.refs_0_, f32[512,4096]{1,0:T(8,128)} %refs_1_.29, f32[512,256]{1,0:T(8,128)} %copy-done.81, f32[512,256]{1,0:T(8,128)} %copy-done.88, ...), custom_call_target="tpu_custom_call", output_to_operand_aliasing={{2}: (14, {})} | custom-call | flops 22020096 | bytes 31457280 | tf_op jit(solution)/shard_map/jit(run_tiles)/pallas_call | solution.py:247
  441.5 5.6 %run_tiles.17 = (f32[2,512,128]{2,1,0:T(8,128)S(1)}, f32[512,4096]{1,0:T(8,128)}) custom-call(s32[1]{0:T(128)} %constant.81.clone.1.refs_0_, f32[512,4096]{1,0:T(8,128)} %refs_1_.29, f32[512,256]{1,0:T(8,128)} %copy-done.83, f32[512,256]{1,0:T(8,128)} %copy-done.94, f32[512,256]{1,0:T(8,128)} %copy-done.45, ...), custom_call_target="tpu_custom_call", output_to_operand_aliasing={{1}: (12, {})} | custom-call | flops 11010048 | bytes 15728640 | tf_op jit(solution)/shard_map/jit(run_tiles)/pallas_call | solution.py:247
  448.7 7.4 %run_tiles.18 = (f32[2,512,128]{2,1,0:T(8,128)S(1)}, f32[512,4096]{1,0:T(8,128)}) custom-call(s32[1]{0:T(128)} %constant.28.clone.1.refs_0_, f32[512,4096]{1,0:T(8,128)} %refs_1_.29, f32[512,256]{1,0:T(8,128)} %copy-done.45, f32[512,256]{1,0:T(8,128)} %copy-done.46, f32[512,256]{1,0:T(8,128)} %copy-done.43, ...), custom_call_target="tpu_custom_call", output_to_operand_aliasing={{1}: (18, {})} | custom-call | flops 18350080 | bytes 26214400 | tf_op jit(solution)/shard_map/jit(run_tiles)/pallas_call | solution.py:247
  457.6 4.4 run_tiles.19
  (441 shorter events, 99.8 us)
Async XLA Ops:
  10.5 24.2 %collective-permute-start.1 = (f32[512,256]{1,0:T(8,128)}, f32[512,256]{1,0:T(8,128)S(1)}, u32[]{:S(2)}, u32[]{:S(2)}) collective-permute-start(f32[512,256]{1,0:T(8,128)} %get-tuple-element.323), channel_id=1, source_target_pairs={{0,8},{8,0},{16,24},{24,16},{1,9},{9,1},{17,25},{25,17},{2,10},{10... | collective-permute-start | bytes 1572872 | tf_op jit(solution)/shard_map/ppermute | solution.py:377
  23.5 22.5 %collective-permute-start.4 = (f32[512,256]{1,0:T(8,128)}, f32[512,256]{1,0:T(8,128)S(1)}, u32[]{:S(2)}, u32[]{:S(2)}) collective-permute-start(f32[512,256]{1,0:T(8,128)} %get-tuple-element.149), channel_id=1, source_target_pairs={{0,8},{8,0},{16,24},{24,16},{1,9},{9,1},{17,25},{25,17},{2,10},{10... | collective-permute-start | bytes 1572872 | tf_op jit(solution)/shard_map/ppermute | solution.py:377
  34.7 22.5 %collective-permute-start.2 = (f32[512,256]{1,0:T(8,128)}, f32[512,256]{1,0:T(8,128)S(1)}, u32[]{:S(2)}, u32[]{:S(2)}) collective-permute-start(f32[512,256]{1,0:T(8,128)} %get-tuple-element.147), channel_id=1, source_target_pairs={{0,8},{8,0},{16,24},{24,16},{1,9},{9,1},{17,25},{25,17},{2,10},{10... | collective-permute-start | bytes 1572872 | tf_op jit(solution)/shard_map/ppermute | solution.py:377
  36.8 27.9 %collective-permute-start.5 = (f32[512,256]{1,0:T(8,128)S(1)}, f32[512,256]{1,0:T(8,128)S(1)}, u32[]{:S(2)}, u32[]{:S(2)}) collective-permute-start(f32[512,256]{1,0:T(8,128)S(1)} %collective-permute-done.refs_2_.refs_7_), channel_id=1, source_target_pairs={{0,16},{24,8},{1,17},{25,9},{2,18},{26,10},{3,19},{27,11},{4,20},{... | collective-permute-start | bytes 1572872 | tf_op jit(solution)/shard_map/ppermute | solution.py:378
  40.2 20.1 %collective-permute-start.6 = (f32[512,256]{1,0:T(8,128)S(1)}, f32[512,256]{1,0:T(8,128)S(1)}, u32[]{:S(2)}, u32[]{:S(2)}) collective-permute-start(f32[512,256]{1,0:T(8,128)S(1)} %collective-permute-done.1.refs_4_.refs_9_), channel_id=1, source_target_pairs={{0,16},{24,8},{1,17},{25,9},{2,18},{26,10},{3,19},{27,11},{4,20},{... | collective-permute-start | bytes 1572872 | tf_op jit(solution)/shard_map/ppermute | solution.py:378
  46.8 21.7 %collective-permute-start.10 = (f32[512,256]{1,0:T(8,128)}, f32[512,256]{1,0:T(8,128)S(1)}, u32[]{:S(2)}, u32[]{:S(2)}) collective-permute-start(f32[512,256]{1,0:T(8,128)} %get-tuple-element.156), channel_id=1, source_target_pairs={{0,8},{8,0},{16,24},{24,16},{1,9},{9,1},{17,25},{25,17},{2,10},{10... | collective-permute-start | bytes 1572872 | tf_op jit(solution)/shard_map/ppermute | solution.py:377
  53.2 61.5 %collective-permute-start.19 = (f32[512,512]{1,0:T(8,128)S(1)}, f32[512,512]{1,0:T(8,128)S(1)}, u32[]{:S(2)}, u32[]{:S(2)}) collective-permute-start(f32[512,512]{1,0:T(8,128)S(1)} %get-tuple-element.172), channel_id=1, source_target_pairs={{0,1},{1,2},{2,3},{3,4},{4,5},{5,6},{6,7},{7,0},{8,9},{9,10},{10,1... | collective-permute-start | bytes 3145736 | tf_op jit(solution)/shard_map/ppermute | solution.py:432
  57.2 26.9 %collective-permute-start.3 = (f32[512,256]{1,0:T(8,128)S(1)}, f32[512,256]{1,0:T(8,128)S(1)}, u32[]{:S(2)}, u32[]{:S(2)}) collective-permute-start(f32[512,256]{1,0:T(8,128)S(1)} %copy-done.134), channel_id=1, source_target_pairs={{0,8},{8,0},{16,24},{24,16},{1,9},{9,1},{17,25},{25,17},{2,10},{10... | collective-permute-start | bytes 1572872 | tf_op jit(solution)/shard_map/ppermute | solution.py:377
  60.3 28.0 %collective-permute-start.13 = (f32[512,256]{1,0:T(8,128)S(1)}, f32[512,256]{1,0:T(8,128)S(1)}, u32[]{:S(2)}, u32[]{:S(2)}) collective-permute-start(f32[512,256]{1,0:T(8,128)S(1)} %collective-permute-done.2.refs_6_.refs_2_), channel_id=1, source_target_pairs={{0,16},{24,8},{1,17},{25,9},{2,18},{26,10},{3,19},{27,11},{4,20},{... | collective-permute-start | bytes 1572872 | tf_op jit(solution)/shard_map/ppermute | solution.py:378
  64.8 19.4 %collective-permute-start.14 = (f32[512,256]{1,0:T(8,128)S(1)}, f32[512,256]{1,0:T(8,128)S(1)}, u32[]{:S(2)}, u32[]{:S(2)}) collective-permute-start(f32[512,256]{1,0:T(8,128)S(1)} %copy-done.105), channel_id=1, source_target_pairs={{0,16},{24,8},{1,17},{25,9},{2,18},{26,10},{3,19},{27,11},{4,20},{... | collective-permute-start | bytes 1572872 | tf_op jit(solution)/shard_map/ppermute | solution.py:378
  68.4 24.2 %collective-permute-start.11 = (f32[512,256]{1,0:T(8,128)S(1)}, f32[512,256]{1,0:T(8,128)S(1)}, u32[]{:S(2)}, u32[]{:S(2)}) collective-permute-start(f32[512,256]{1,0:T(8,128)S(1)} %copy-done.133), channel_id=1, source_target_pairs={{0,8},{8,0},{16,24},{24,16},{1,9},{9,1},{17,25},{25,17},{2,10},{10... | collective-permute-start | bytes 1572872 | tf_op jit(solution)/shard_map/ppermute | solution.py:377
  84.2 20.0 %collective-permute-start.15 = (f32[512,256]{1,0:T(8,128)S(1)}, f32[512,256]{1,0:T(8,128)S(1)}, u32[]{:S(2)}, u32[]{:S(2)}) collective-permute-start(f32[512,256]{1,0:T(8,128)S(1)} %collective-permute-done.10.refs_8_.refs_4_), channel_id=1, source_target_pairs={{0,16},{24,8},{1,17},{25,9},{2,18},{26,10},{3,19},{27,11},{4,20},{... | collective-permute-start | bytes 1572872 | tf_op jit(solution)/shard_map/ppermute | solution.py:378
  88.3 22.0 %collective-permute-start.17 = (f32[512,256]{1,0:T(8,128)S(1)}, f32[512,256]{1,0:T(8,128)S(1)}, u32[]{:S(2)}, u32[]{:S(2)}) collective-permute-start(f32[512,256]{1,0:T(8,128)S(1)} %collective-permute-done.3.refs_7_), channel_id=1, source_target_pairs={{0,16},{24,8},{1,17},{25,9},{2,18},{26,10},{3,19},{27,11},{4,20},{... | collective-permute-start | bytes 1572872 | tf_op jit(solution)/shard_map/ppermute | solution.py:378
  92.6 22.1 %collective-permute-start.12 = (f32[512,256]{1,0:T(8,128)S(1)}, f32[512,256]{1,0:T(8,128)}, u32[]{:S(2)}, u32[]{:S(2)}) collective-permute-start(f32[512,256]{1,0:T(8,128)S(1)} %get-tuple-element.158), channel_id=1, source_target_pairs={{0,8},{8,0},{16,24},{24,16},{1,9},{9,1},{17,25},{25,17},{2,10},{10... | collective-permute-start | bytes 1572872 | tf_op jit(solution)/shard_map/ppermute | solution.py:377
  102.1 24.3 %collective-permute-start.8 = (f32[512,256]{1,0:T(8,128)S(1)}, f32[512,256]{1,0:T(8,128)S(1)}, u32[]{:S(2)}, u32[]{:S(2)}) collective-permute-start(f32[512,256]{1,0:T(8,128)S(1)} %copy-done.131), channel_id=1, source_target_pairs={{0,8},{8,0},{16,24},{24,16},{1,9},{9,1},{17,25},{25,17},{2,10},{10... | collective-permute-start | bytes 1572872 | tf_op jit(solution)/shard_map/ppermute | solution.py:377
  104.2 22.6 %collective-permute-start.16 = (f32[512,256]{1,0:T(8,128)S(1)}, f32[512,256]{1,0:T(8,128)S(1)}, u32[]{:S(2)}, u32[]{:S(2)}) collective-permute-start(f32[512,256]{1,0:T(8,128)S(1)} %collective-permute-done.11.refs_6_.refs_2_), channel_id=1, source_target_pairs={{0,16},{24,8},{1,17},{25,9},{2,18},{26,10},{3,19},{27,11},{4,20},{... | collective-permute-start | bytes 1572872 | tf_op jit(solution)/shard_map/ppermute | solution.py:378
  110.3 20.0 %collective-permute-start.18 = (f32[512,256]{1,0:T(8,128)S(1)}, f32[512,256]{1,0:T(8,128)S(1)}, u32[]{:S(2)}, u32[]{:S(2)}) collective-permute-start(f32[512,256]{1,0:T(8,128)S(1)} %collective-permute-done.7.refs_8_.refs_4_), channel_id=1, source_target_pairs={{0,16},{24,8},{1,17},{25,9},{2,18},{26,10},{3,19},{27,11},{4,20},{... | collective-permute-start | bytes 1572872 | tf_op jit(solution)/shard_map/ppermute | solution.py:378
  114.7 20.0 %collective-permute-start.20 = (f32[512,256]{1,0:T(8,128)S(1)}, f32[512,256]{1,0:T(8,128)S(1)}, u32[]{:S(2)}, u32[]{:S(2)}) collective-permute-start(f32[512,256]{1,0:T(8,128)S(1)} %collective-permute-done.3.refs_7_), channel_id=1, source_target_pairs={{0,1},{1,2},{2,3},{3,4},{4,5},{5,6},{6,7},{7,0},{8,9},{9,10},{10,1... | collective-permute-start | bytes 1572872 | tf_op jit(solution)/shard_map/ppermute | solution.py:441
  114.8 21.2 %collective-permute-start.21 = (f32[512,256]{1,0:T(8,128)S(1)}, f32[512,256]{1,0:T(8,128)S(1)}, u32[]{:S(2)}, u32[]{:S(2)}) collective-permute-start(f32[512,256]{1,0:T(8,128)S(1)} %collective-permute-done.17.refs_8_), channel_id=1, source_target_pairs={{0,1},{1,2},{2,3},{3,4},{4,5},{5,6},{6,7},{7,0},{8,9},{9,10},{10,1... | collective-permute-start | bytes 1572872 | tf_op jit(solution)/shard_map/ppermute | solution.py:441
  126.4 19.7 %collective-permute-start.25 = (f32[512,256]{1,0:T(8,128)S(1)}, f32[512,256]{1,0:T(8,128)S(1)}, u32[]{:S(2)}, u32[]{:S(2)}) collective-permute-start(f32[512,256]{1,0:T(8,128)S(1)} %copy-done.129), channel_id=1, source_target_pairs={{0,8},{8,0},{16,24},{24,16},{1,9},{9,1},{17,25},{25,17},{2,10},{10... | collective-permute-start | bytes 1572872 | tf_op jit(solution)/shard_map/ppermute | solution.py:377
  126.8 29.3 %collective-permute-start.9 = (f32[512,256]{1,0:T(8,128)S(1)}, f32[512,256]{1,0:T(8,128)S(1)}, u32[]{:S(2)}, u32[]{:S(2)}) collective-permute-start(f32[512,256]{1,0:T(8,128)S(1)} %get-tuple-element.155), channel_id=1, source_target_pairs={{0,8},{8,0},{16,24},{24,16},{1,9},{9,1},{17,25},{25,17},{2,10},{10... | collective-permute-start | bytes 1572872 | tf_op jit(solution)/shard_map/ppermute | solution.py:377
  130.3 28.0 %collective-permute-start.29 = (f32[512,256]{1,0:T(8,128)}, f32[512,256]{1,0:T(8,128)S(1)}, u32[]{:S(2)}, u32[]{:S(2)}) collective-permute-start(f32[512,256]{1,0:T(8,128)} %collective-permute-done.12.refs_5_.refs_4_), channel_id=1, source_target_pairs={{0,16},{24,8},{1,17},{25,9},{2,18},{26,10},{3,19},{27,11},{4,20},{... | collective-permute-start | bytes 1572872 | tf_op jit(solution)/shard_map/ppermute | solution.py:378
  134.7 25.3 %collective-permute-start.28 = (f32[512,256]{1,0:T(8,128)S(1)}, f32[512,256]{1,0:T(8,128)S(1)}, u32[]{:S(2)}, u32[]{:S(2)}) collective-permute-start(f32[512,256]{1,0:T(8,128)S(1)} %collective-permute-done.8.refs_6_.refs_2_), channel_id=1, source_target_pairs={{0,16},{24,8},{1,17},{25,9},{2,18},{26,10},{3,19},{27,11},{4,20},{... | collective-permute-start | bytes 1572872 | tf_op jit(solution)/shard_map/ppermute | solution.py:378
  156.1 18.9 %collective-permute-start.22 = (f32[512,256]{1,0:T(8,128)S(1)}, f32[512,256]{1,0:T(8,128)S(1)}, u32[]{:S(2)}, u32[]{:S(2)}) collective-permute-start(f32[512,256]{1,0:T(8,128)S(1)} %copy-done.124), channel_id=1, source_target_pairs={{0,8},{8,0},{16,24},{24,16},{1,9},{9,1},{17,25},{25,17},{2,10},{10... | collective-permute-start | bytes 1572872 | tf_op jit(solution)/shard_map/ppermute | solution.py:377
  161.6 49.2 %collective-permute-start.43 = (f32[512,512]{1,0:T(8,128)S(1)}, f32[512,512]{1,0:T(8,128)S(1)}, u32[]{:S(2)}, u32[]{:S(2)}) collective-permute-start(f32[512,512]{1,0:T(8,128)S(1)} %get-tuple-element.209), channel_id=1, source_target_pairs={{0,1},{1,2},{2,3},{3,4},{4,5},{5,6},{6,7},{7,0},{8,9},{9,10},{10,1... | collective-permute-start | bytes 3145736 | tf_op jit(solution)/shard_map/ppermute | solution.py:432
  163.8 22.5 %collective-permute-start.27 = (f32[512,256]{1,0:T(8,128)S(1)}, f32[512,256]{1,0:T(8,128)S(1)}, u32[]{:S(2)}, u32[]{:S(2)}) collective-permute-start(f32[512,256]{1,0:T(8,128)S(1)} %copy-done.123), channel_id=1, source_target_pairs={{0,8},{8,0},{16,24},{24,16},{1,9},{9,1},{17,25},{25,17},{2,10},{10... | collective-permute-start | bytes 1572872 | tf_op jit(solution)/shard_map/ppermute | solution.py:377
  175.0 36.5 %collective-permute-start.47 = (f32[512,512]{1,0:T(8,128)S(1)}, f32[512,512]{1,0:T(8,128)S(1)}, u32[]{:S(2)}, u32[]{:S(2)}) collective-permute-start(f32[512,512]{1,0:T(8,128)S(1)} %get-tuple-element.226), channel_id=1, source_target_pairs={{1,0},{2,1},{3,2},{4,3},{5,4},{6,5},{7,6},{0,7},{9,8},{10,9},{11,1... | collective-permute-start | bytes 3145736 | tf_op jit(solution)/shard_map/ppermute | solution.py:432
  175.1 21.4 %collective-permute-start.23 = (f32[512,256]{1,0:T(8,128)S(1)}, f32[512,256]{1,0:T(8,128)S(1)}, u32[]{:S(2)}, u32[]{:S(2)}) collective-permute-start(f32[512,256]{1,0:T(8,128)S(1)} %copy-done.122), channel_id=1, source_target_pairs={{0,8},{8,0},{16,24},{24,16},{1,9},{9,1},{17,25},{25,17},{2,10},{10... | collective-permute-start | bytes 1572872 | tf_op jit(solution)/shard_map/ppermute | solution.py:377
  186.3 22.5 %collective-permute-start.33 = (f32[512,256]{1,0:T(8,128)S(1)}, f32[512,256]{1,0:T(8,128)S(1)}, u32[]{:S(2)}, u32[]{:S(2)}) collective-permute-start(f32[512,256]{1,0:T(8,128)S(1)} %collective-permute-done.22.refs_8_.refs_4_), channel_id=1, source_target_pairs={{0,16},{24,8},{1,17},{25,9},{2,18},{26,10},{3,19},{27,11},{4,20},{... | collective-permute-start | bytes 1572872 | tf_op jit(solution)/shard_map/ppermute | solution.py:378
  196.5 19.3 %collective-permute-start.45 = (f32[512,256]{1,0:T(8,128)S(1)}, f32[512,256]{1,0:T(8,128)S(1)}, u32[]{:S(2)}, u32[]{:S(2)}) collective-permute-start(f32[512,256]{1,0:T(8,128)S(1)} %collective-permute-done.32.refs_4_.refs_9_.refs_7_), channel_id=1, source_target_pairs={{0,1},{1,2},{2,3},{3,4},{4,5},{5,6},{6,7},{7,0},{8,9},{9,10},{10,1... | collective-permute-start | bytes 1572872 | tf_op jit(solution)/shard_map/ppermute | solution.py:441
  208.8 40.2 %collective-permute-start.48 = (f32[512,256]{1,0:T(8,128)}, f32[512,256]{1,0:T(8,128)}, u32[]{:S(2)}, u32[]{:S(2)}) collective-permute-start(f32[512,256]{1,0:T(8,128)} %collective-permute-done.12.refs_5_.refs_4_), channel_id=1, source_target_pairs={{1,0},{2,1},{3,2},{4,3},{5,4},{6,5},{7,6},{0,7},{9,8},{10,9},{11,1... | collective-permute-start | bytes 1572872 | tf_op jit(solution)/shard_map/ppermute | solution.py:441
  211.5 32.4 %collective-permute-start.36 = (f32[512,256]{1,0:T(8,128)}, f32[512,256]{1,0:T(8,128)S(1)}, u32[]{:S(2)}, u32[]{:S(2)}) collective-permute-start(f32[512,256]{1,0:T(8,128)} %get-tuple-element.201), channel_id=1, source_target_pairs={{0,8},{8,0},{16,24},{24,16},{1,9},{9,1},{17,25},{25,17},{2,10},{10... | collective-permute-start | bytes 1572872 | tf_op jit(solution)/shard_map/ppermute | solution.py:377
  212.9 31.8 %collective-permute-start.37 = (f32[512,256]{1,0:T(8,128)S(1)}, f32[512,256]{1,0:T(8,128)S(1)}, u32[]{:S(2)}, u32[]{:S(2)}) collective-permute-start(f32[512,256]{1,0:T(8,128)S(1)} %collective-permute-done.27.refs_6_.refs_2_), channel_id=1, source_target_pairs={{0,16},{24,8},{1,17},{25,9},{2,18},{26,10},{3,19},{27,11},{4,20},{... | collective-permute-start | bytes 1572872 | tf_op jit(solution)/shard_map/ppermute | solution.py:378
  215.8 30.3 %collective-permute-start.39 = (f32[512,256]{1,0:T(8,128)S(1)}, f32[512,256]{1,0:T(8,128)S(1)}, u32[]{:S(2)}, u32[]{:S(2)}) collective-permute-start(f32[512,256]{1,0:T(8,128)S(1)} %collective-permute-done.23.refs_8_.refs_4_), channel_id=1, source_target_pairs={{0,16},{24,8},{1,17},{25,9},{2,18},{26,10},{3,19},{27,11},{4,20},{... | collective-permute-start | bytes 1572872 | tf_op jit(solution)/shard_map/ppermute | solution.py:378
  225.9 24.5 %collective-permute-start.49 = (f32[512,256]{1,0:T(8,128)}, f32[512,256]{1,0:T(8,128)S(1)}, u32[]{:S(2)}, u32[]{:S(2)}) collective-permute-start(f32[512,256]{1,0:T(8,128)} %copy-done.72), channel_id=1, source_target_pairs={{1,0},{2,1},{3,2},{4,3},{5,4},{6,5},{7,6},{0,7},{9,8},{10,9},{11,1... | collective-permute-start | bytes 1572872 | tf_op jit(solution)/shard_map/ppermute | solution.py:441
  243.9 23.5 %collective-permute-start.34 = (f32[512,256]{1,0:T(8,128)S(1)}, f32[512,256]{1,0:T(8,128)S(1)}, u32[]{:S(2)}, u32[]{:S(2)}) collective-permute-start(f32[512,256]{1,0:T(8,128)S(1)} %copy-done.130), channel_id=1, source_target_pairs={{0,8},{8,0},{16,24},{24,16},{1,9},{9,1},{17,25},{25,17},{2,10},{10... | collective-permute-start | bytes 1572872 | tf_op jit(solution)/shard_map/ppermute | solution.py:377
  244.7 24.9 %collective-permute-start.46 = (f32[512,256]{1,0:T(8,128)S(1)}, f32[512,256]{1,0:T(8,128)S(1)}, u32[]{:S(2)}, u32[]{:S(2)}) collective-permute-start(f32[512,256]{1,0:T(8,128)S(1)} %copy-done.128), channel_id=1, source_target_pairs={{0,8},{8,0},{16,24},{24,16},{1,9},{9,1},{17,25},{25,17},{2,10},{10... | collective-permute-start | bytes 1572872 | tf_op jit(solution)/shard_map/ppermute | solution.py:377
  246.1 24.2 %collective-permute-start.38 = (f32[512,256]{1,0:T(8,128)S(1)}, f32[512,256]{1,0:T(8,128)S(1)}, u32[]{:S(2)}, u32[]{:S(2)}) collective-permute-start(f32[512,256]{1,0:T(8,128)S(1)} %collective-permute-done.36.refs_3_.refs_6_), channel_id=1, source_target_pairs={{0,16},{24,8},{1,17},{25,9},{2,18},{26,10},{3,19},{27,11},{4,20},{... | collective-permute-start | bytes 1572872 | tf_op jit(solution)/shard_map/ppermute | solution.py:378
  249.0 25.7 %collective-permute-start.40 = (f32[512,256]{1,0:T(8,128)S(1)}, f32[512,256]{1,0:T(8,128)S(1)}, u32[]{:S(2)}, u32[]{:S(2)}) collective-permute-start(f32[512,256]{1,0:T(8,128)S(1)} %collective-permute-done.24.refs_5_.refs_8_), channel_id=1, source_target_pairs={{0,16},{24,8},{1,17},{25,9},{2,18},{26,10},{3,19},{27,11},{4,20},{... | collective-permute-start | bytes 1572872 | tf_op jit(solution)/shard_map/ppermute | solution.py:378
  250.4 60.9 %collective-permute-start.35 = (f32[512,512]{1,0:T(8,128)S(1)}, f32[512,512]{1,0:T(8,128)S(1)}, u32[]{:S(2)}, u32[]{:S(2)}) collective-permute-start(f32[512,512]{1,0:T(8,128)S(1)} %copy-done.103), channel_id=1, source_target_pairs={{1,0},{2,1},{3,2},{4,3},{5,4},{6,5},{7,6},{0,7},{9,8},{10,9},{11,1... | collective-permute-start | bytes 3145736 | tf_op jit(solution)/shard_map/ppermute | solution.py:432
  269.6 22.8 %collective-permute-start.50 = (f32[512,256]{1,0:T(8,128)S(1)}, f32[512,256]{1,0:T(8,128)S(1)}, u32[]{:S(2)}, u32[]{:S(2)}) collective-permute-start(f32[512,256]{1,0:T(8,128)S(1)} %copy-done.126), channel_id=1, source_target_pairs={{0,8},{8,0},{16,24},{24,16},{1,9},{9,1},{17,25},{25,17},{2,10},{10... | collective-permute-start | bytes 1572872 | tf_op jit(solution)/shard_map/ppermute | solution.py:377
  270.3 23.4 %collective-permute-start.57 = (f32[512,256]{1,0:T(8,128)S(1)}, f32[512,256]{1,0:T(8,128)S(1)}, u32[]{:S(2)}, u32[]{:S(2)}) collective-permute-start(f32[512,256]{1,0:T(8,128)S(1)} %collective-permute-done.46.refs_6_.refs_2_), channel_id=1, source_target_pairs={{0,16},{24,8},{1,17},{25,9},{2,18},{26,10},{3,19},{27,11},{4,20},{... | collective-permute-start | bytes 1572872 | tf_op jit(solution)/shard_map/ppermute | solution.py:378
  274.8 21.2 %collective-permute-start.65 = (f32[512,256]{1,0:T(8,128)S(1)}, f32[512,256]{1,0:T(8,128)S(1)}, u32[]{:S(2)}, u32[]{:S(2)}) collective-permute-start(f32[512,256]{1,0:T(8,128)S(1)} %collective-permute-done.34.refs_8_.refs_4_), channel_id=1, source_target_pairs={{0,16},{24,8},{1,17},{25,9},{2,18},{26,10},{3,19},{27,11},{4,20},{... | collective-permute-start | bytes 1572872 | tf_op jit(solution)/shard_map/ppermute | solution.py:378
  282.3 29.0 %collective-permute-start.41 = (f32[512,256]{1,0:T(8,128)S(1)}, f32[512,256]{1,0:T(8,128)S(1)}, u32[]{:S(2)}, u32[]{:S(2)}) collective-permute-start(f32[512,256]{1,0:T(8,128)S(1)} %copy-done.106), channel_id=1, source_target_pairs={{1,0},{2,1},{3,2},{4,3},{5,4},{6,5},{7,6},{0,7},{9,8},{10,9},{11,1... | collective-permute-start | bytes 1572872 | tf_op jit(solution)/shard_map/ppermute | solution.py:441
  292.4 22.5 %collective-permute-start.42 = (f32[512,256]{1,0:T(8,128)S(1)}, f32[512,256]{1,0:T(8,128)S(1)}, u32[]{:S(2)}, u32[]{:S(2)}) collective-permute-start(f32[512,256]{1,0:T(8,128)S(1)} %copy-done.109), channel_id=1, source_target_pairs={{1,0},{2,1},{3,2},{4,3},{5,4},{6,5},{7,6},{0,7},{9,8},{10,9},{11,1... | collective-permute-start | bytes 1572872 | tf_op jit(solution)/shard_map/ppermute | solution.py:441
  293.7 31.0 %collective-permute-start.51 = (f32[512,256]{1,0:T(8,128)S(1)}, f32[512,256]{1,0:T(8,128)S(1)}, u32[]{:S(2)}, u32[]{:S(2)}) collective-permute-start(f32[512,256]{1,0:T(8,128)S(1)} %copy-done.121), channel_id=1, source_target_pairs={{0,8},{8,0},{16,24},{24,16},{1,9},{9,1},{17,25},{25,17},{2,10},{10... | collective-permute-start | bytes 1572872 | tf_op jit(solution)/shard_map/ppermute | solution.py:377
  296.0 28.7 %collective-permute-start.58 = (f32[512,256]{1,0:T(8,128)S(1)}, f32[512,256]{1,0:T(8,128)S(1)}, u32[]{:S(2)}, u32[]{:S(2)}) collective-permute-start(f32[512,256]{1,0:T(8,128)S(1)} %collective-permute-done.50.refs_6_.refs_2_), channel_id=1, source_target_pairs={{0,16},{24,8},{1,17},{25,9},{2,18},{26,10},{3,19},{27,11},{4,20},{... | collective-permute-start | bytes 1572872 | tf_op jit(solution)/shard_map/ppermute | solution.py:378
  311.3 28.4 %collective-permute-start.64 = (f32[512,256]{1,0:T(8,128)S(1)}, f32[512,256]{1,0:T(8,128)S(1)}, u32[]{:S(2)}, u32[]{:S(2)}) collective-permute-start(f32[512,256]{1,0:T(8,128)S(1)} %copy-done.120), channel_id=1, source_target_pairs={{0,8},{8,0},{16,24},{24,16},{1,9},{9,1},{17,25},{25,17},{2,10},{10... | collective-permute-start | bytes 1572872 | tf_op jit(solution)/shard_map/ppermute | solution.py:377
  311.4 28.4 %collective-permute-start.67 = (f32[512,256]{1,0:T(8,128)S(1)}, f32[512,256]{1,0:T(8,128)S(1)}, u32[]{:S(2)}, u32[]{:S(2)}) collective-permute-start(f32[512,256]{1,0:T(8,128)S(1)} %collective-permute-done.63.refs_8_.refs_4_), channel_id=1, source_target_pairs={{0,16},{24,8},{1,17},{25,9},{2,18},{26,10},{3,19},{27,11},{4,20},{... | collective-permute-start | bytes 1572872 | tf_op jit(solution)/shard_map/ppermute | solution.py:378
  339.7 18.9 %collective-permute-start.66 = (f32[512,256]{1,0:T(8,128)S(1)}, f32[512,256]{1,0:T(8,128)S(1)}, u32[]{:S(2)}, u32[]{:S(2)}) collective-permute-start(f32[512,256]{1,0:T(8,128)S(1)} %copy-done.118), channel_id=1, source_target_pairs={{0,8},{8,0},{16,24},{24,16},{1,9},{9,1},{17,25},{25,17},{2,10},{10... | collective-permute-start | bytes 1572872 | tf_op jit(solution)/shard_map/ppermute | solution.py:377
  343.3 22.6 %collective-permute-start.53 = (f32[512,256]{1,0:T(8,128)S(1)}, f32[512,256]{1,0:T(8,128)S(1)}, u32[]{:S(2)}, u32[]{:S(2)}) collective-permute-start(f32[512,256]{1,0:T(8,128)S(1)} %copy-done.117), channel_id=1, source_target_pairs={{0,8},{8,0},{16,24},{24,16},{1,9},{9,1},{17,25},{25,17},{2,10},{10... | collective-permute-start | bytes 1572872 | tf_op jit(solution)/shard_map/ppermute | solution.py:377
  343.4 23.4 %collective-permute-start.60 = (f32[512,256]{1,0:T(8,128)S(1)}, f32[512,256]{1,0:T(8,128)S(1)}, u32[]{:S(2)}, u32[]{:S(2)}) collective-permute-start(f32[512,256]{1,0:T(8,128)S(1)} %collective-permute-done.52.refs_6_.refs_2_), channel_id=1, source_target_pairs={{0,16},{24,8},{1,17},{25,9},{2,18},{26,10},{3,19},{27,11},{4,20},{... | collective-permute-start | bytes 1572872 | tf_op jit(solution)/shard_map/ppermute | solution.py:378
  358.6 23.2 %collective-permute-start.70 = (f32[512,256]{1,0:T(8,128)S(1)}, f32[512,256]{1,0:T(8,128)S(1)}, u32[]{:S(2)}, u32[]{:S(2)}) collective-permute-start(f32[512,256]{1,0:T(8,128)S(1)} %copy-done.116), channel_id=1, source_target_pairs={{0,8},{8,0},{16,24},{24,16},{1,9},{9,1},{17,25},{25,17},{2,10},{10... | collective-permute-start | bytes 1572872 | tf_op jit(solution)/shard_map/ppermute | solution.py:377
  358.7 23.2 %collective-permute-start.69 = (f32[512,256]{1,0:T(8,128)S(1)}, f32[512,256]{1,0:T(8,128)S(1)}, u32[]{:S(2)}, u32[]{:S(2)}) collective-permute-start(f32[512,256]{1,0:T(8,128)S(1)} %collective-permute-done.66.refs_8_.refs_4_), channel_id=1, source_target_pairs={{0,16},{24,8},{1,17},{25,9},{2,18},{26,10},{3,19},{27,11},{4,20},{... | collective-permute-start | bytes 1572872 | tf_op jit(solution)/shard_map/ppermute | solution.py:378
  365.9 22.5 %collective-permute-start.54 = (f32[512,256]{1,0:T(8,128)S(1)}, f32[512,256]{1,0:T(8,128)S(1)}, u32[]{:S(2)}, u32[]{:S(2)}) collective-permute-start(f32[512,256]{1,0:T(8,128)S(1)} %copy-done.115), channel_id=1, source_target_pairs={{0,8},{8,0},{16,24},{24,16},{1,9},{9,1},{17,25},{25,17},{2,10},{10... | collective-permute-start | bytes 1572872 | tf_op jit(solution)/shard_map/ppermute | solution.py:377
  366.9 22.5 %collective-permute-start.61 = (f32[512,256]{1,0:T(8,128)S(1)}, f32[512,256]{1,0:T(8,128)S(1)}, u32[]{:S(2)}, u32[]{:S(2)}) collective-permute-start(f32[512,256]{1,0:T(8,128)S(1)} %collective-permute-done.53.refs_6_.refs_2_), channel_id=1, source_target_pairs={{0,16},{24,8},{1,17},{25,9},{2,18},{26,10},{3,19},{27,11},{4,20},{... | collective-permute-start | bytes 1572872 | tf_op jit(solution)/shard_map/ppermute | solution.py:378
  381.9 25.4 %collective-permute-start.73 = (f32[512,256]{1,0:T(8,128)}, f32[512,256]{1,0:T(8,128)S(1)}, u32[]{:S(2)}, u32[]{:S(2)}) collective-permute-start(f32[512,256]{1,0:T(8,128)} %get-tuple-element.273), channel_id=1, source_target_pairs={{0,8},{8,0},{16,24},{24,16},{1,9},{9,1},{17,25},{25,17},{2,10},{10... | collective-permute-start | bytes 1572872 | tf_op jit(solution)/shard_map/ppermute | solution.py:377
  381.9 25.4 %collective-permute-start.71 = (f32[512,256]{1,0:T(8,128)S(1)}, f32[512,256]{1,0:T(8,128)}, u32[]{:S(2)}, u32[]{:S(2)}) collective-permute-start(f32[512,256]{1,0:T(8,128)S(1)} %collective-permute-done.70.refs_8_.refs_4_), channel_id=1, source_target_pairs={{0,16},{24,8},{1,17},{25,9},{2,18},{26,10},{3,19},{27,11},{4,20},{... | collective-permute-start | bytes 1572872 | tf_op jit(solution)/shard_map/ppermute | solution.py:378
  388.4 31.0 %collective-permute-start.55 = (f32[512,256]{1,0:T(8,128)}, f32[512,256]{1,0:T(8,128)S(1)}, u32[]{:S(2)}, u32[]{:S(2)}) collective-permute-start(f32[512,256]{1,0:T(8,128)} %get-tuple-element.235), channel_id=1, source_target_pairs={{0,8},{8,0},{16,24},{24,16},{1,9},{9,1},{17,25},{25,17},{2,10},{10... | collective-permute-start | bytes 1572872 | tf_op jit(solution)/shard_map/ppermute | solution.py:377
  389.3 30.0 %collective-permute-start.62 = (f32[512,256]{1,0:T(8,128)S(1)}, f32[512,256]{1,0:T(8,128)S(1)}, u32[]{:S(2)}, u32[]{:S(2)}) collective-permute-start(f32[512,256]{1,0:T(8,128)S(1)} %collective-permute-done.54.refs_2_.refs_6_), channel_id=1, source_target_pairs={{0,16},{24,8},{1,17},{25,9},{2,18},{26,10},{3,19},{27,11},{4,20},{... | collective-permute-start | bytes 1572872 | tf_op jit(solution)/shard_map/ppermute | solution.py:378
  407.3 19.8 %collective-permute-start.75 = (f32[512,256]{1,0:T(8,128)S(1)}, f32[512,256]{1,0:T(8,128)S(1)}, u32[]{:S(2)}, u32[]{:S(2)}) collective-permute-start(f32[512,256]{1,0:T(8,128)S(1)} %collective-permute-done.73.refs_4_.refs_2_.refs_8_), channel_id=1, source_target_pairs={{0,16},{24,8},{1,17},{25,9},{2,18},{26,10},{3,19},{27,11},{4,20},{... | collective-permute-start | bytes 1572872 | tf_op jit(solution)/shard_map/ppermute | solution.py:378
  419.4 20.5 %collective-permute-start.72 = (f32[512,256]{1,0:T(8,128)S(1)}, f32[512,256]{1,0:T(8,128)S(1)}, u32[]{:S(2)}, u32[]{:S(2)}) collective-permute-start(f32[512,256]{1,0:T(8,128)S(1)} %collective-permute-done.55.refs_6_.refs_4_.refs_2_), channel_id=1, source_target_pairs={{0,16},{24,8},{1,17},{25,9},{2,18},{26,10},{3,19},{27,11},{4,20},{... | collective-permute-start | bytes 1572872 | tf_op jit(solution)/shard_map/ppermute | solution.py:378
  420.8 19.1 %collective-permute-start.56 = (f32[256,256]{1,0:T(8,128)S(1)}, f32[256,256]{1,0:T(8,128)S(1)}, u32[]{:S(2)}, u32[]{:S(2)}) collective-permute-start(f32[256,256]{1,0:T(8,128)S(1)} %get-tuple-element.236), channel_id=1, source_target_pairs={{0,8},{8,0},{16,24},{24,16},{1,9},{9,1},{17,25},{25,17},{2,10},{10... | collective-permute-start | bytes 786440 | tf_op jit(solution)/shard_map/ppermute | solution.py:377
  427.1 20.8 %collective-permute-start.76 = (f32[256,256]{1,0:T(8,128)S(1)}, f32[256,256]{1,0:T(8,128)S(1)}, u32[]{:S(2)}, u32[]{:S(2)}) collective-permute-start(f32[256,256]{1,0:T(8,128)S(1)} %collective-permute-done.74.refs_8_), channel_id=1, source_target_pairs={{0,16},{24,8},{1,17},{25,9},{2,18},{26,10},{3,19},{27,11},{4,20},{... | collective-permute-start | bytes 786440 | tf_op jit(solution)/shard_map/ppermute | solution.py:378
  (156 other events, 2319.5 us)
